TPU v7x, 128 devices: a whole 4x4x4 slice. The times are simulated.
128 devices in a mesh: grp: 8 (over z, core), frac: 16 (over y, x).
Axes of the slice: x: 4, y: 4, z: 4, core: 2. Of those that a mesh axis runs over, the one named last changes fastest.
Arguments:
- matrix_state: float32 [2, 1024, 4096], P(None, 'grp', 'frac'), may hold values from 0 to 1
- matrix_perm: float32 [1024, 4096], P('grp', 'frac'), may hold values from 0.1 to 10
- frac_state: float32 [2, 8, 131072], P(None, 'grp', 'frac'), may hold values from 0 to 1
- frac_aperture: float32 [8, 131072], P('grp', 'frac'), may hold values from 0.5 to 4
- link_cell: int32 [8, 16, 16, 256], P('grp', 'frac'), may hold values from 0 to 32767
- link_seg: int32 [8, 16, 16, 256], P('grp', 'frac'), may hold values from 0 to 8191
- link_trans: float32 [8, 16, 16, 256], P('grp', 'frac'), may hold values from 0.1 to 2
- link_count: int32 [8, 16, 16], P('grp', 'frac'), may hold values from 32 to 256, as said below
- link_upwind: int32 [3, 8, 16, 16, 256], P(None, 'grp', 'frac'), may hold values from 0 to 1
Outputs:
- matrix_out: float32 [2, 1024, 4096], P(None, 'grp', 'frac')
- frac_out: float32 [2, 8, 131072], P(None, 'grp', 'frac')
Inputs may be any that keep to these rules, and one draw needn't show every extreme that they name: `link_count`: in each source device's list at least one owner block holds exactly 256 live slots; slots at or beyond a block's count are padding. `link_cell`: A live slot's cell index lies within the source device's 128 x 256 block. `link_seg`: A slot's segment index counts within the owner's 8192 segments. `link_upwind`: 1 takes the upwind saturation from the matrix cell, 0 from the fracture segment.
All inputs are finite; a program needn't handle non-finite values.
Results may differ from a plain program's by a relative error of at most 0.00002.
Values sent between devices are 32-bit elements; how exact they have to be, the bound alone decides.
A program may use at most 128 MiB of HBM per device.

v0:
```python
import jax
import jax.numpy as jnp
from jax import lax
from jax.sharding import PartitionSpec as P

ITERS = 3
SWEEPS = 4


LOW_BOUND = 0.02
HIGH_BOUND = 1.98
TAU_STEP = 0.5
MOBILITY_FLOOR = 0.2


def extended(cells, sides, width):
    for axis, dim in sides:
        count = lax.axis_size(axis)
        ends = count - 1
        head = lax.slice_in_dim(cells, 0, width, axis=dim)
        tail = lax.slice_in_dim(cells, cells.shape[dim] - width, cells.shape[dim], axis=dim)
        cells = jnp.concatenate(
            [
                lax.ppermute(tail, axis, [(i, (i + 1) % count) for i in range(ends)]),
                cells,
                lax.ppermute(head, axis, [((i + 1) % count, i) for i in range(ends)]),
            ],
            axis=dim,
        )
    return cells


def apply_matrix(values, diagonal):
    padded = extended(values, (("grp", 0), ("frac", 1)), 1)
    beside = padded[2:, 1:-1] + padded[:-2, 1:-1] + padded[1:-1, 2:] + padded[1:-1, :-2]
    return diagonal * values - beside


def chebyshev(start_field, right_side, diagonal):
    centre = 0.5 * (HIGH_BOUND + LOW_BOUND)
    half_width = 0.5 * (HIGH_BOUND - LOW_BOUND)
    scale_ratio = centre / half_width
    ratio_now = 1.0 / scale_ratio
    inverse = 1.0 / diagonal
    residual = inverse * (right_side - apply_matrix(start_field, diagonal))
    update = residual / centre
    iterate = start_field
    for sweep_index in range(SWEEPS):
        iterate = iterate + update
        if sweep_index + 1 < SWEEPS:
            residual = inverse * (right_side - apply_matrix(iterate, diagonal))
            ratio_next = 1.0 / (2.0 * scale_ratio - ratio_now)
            update = ratio_next * ratio_now * update + 2.0 * ratio_next / half_width * residual
            ratio_now = ratio_next
    return iterate


def owner_lists(local_segment):
    return lax.all_to_all(local_segment, "frac", split_axis=0, concat_axis=0, tiled=True)


def on_device(
    matrix_state,
    matrix_perm,
    frac_state,
    frac_aperture,
    link_cell,
    link_seg,
    link_trans,
    link_count,
    link_upwind,
):
    members = lax.axis_size("frac")
    position = lax.axis_index("frac")
    cell_index = link_cell[0, 0]
    local_segment = link_seg[0, 0]
    transmit = link_trans[0, 0].reshape(-1)
    block_count = link_count[0, 0]
    upwind_all = link_upwind[:, 0, 0]
    capacity = cell_index.shape[1]
    seg_dev = frac_state.shape[2]
    row_count, column_count = matrix_perm.shape
    live_slots = (
        (jnp.arange(capacity, dtype=jnp.int32)[None, :] < block_count[:, None])
        .astype(jnp.int32)
        .reshape(-1)
    )
    cell_flat = cell_index.reshape(-1)
    global_segment = (
        jnp.arange(members, dtype=jnp.int32)[:, None] * seg_dev + local_segment
    ).reshape(-1)
    pressure = matrix_state[0]
    saturation = matrix_state[1]
    frac_pressure = frac_state[0, 0]
    frac_saturation = frac_state[1, 0]
    aperture = frac_aperture[0]
    targets = None
    targets = owner_lists(local_segment)
    for outer in range(ITERS):
        group_states = lax.all_gather(
            jnp.stack([frac_pressure, frac_saturation]), "frac", axis=1, tiled=True
        )
        seg_pressure = group_states[0][global_segment]
        seg_saturation = group_states[1][global_segment]
        group_length = group_states.shape[1]
        first_segment = position * seg_dev
        before = lax.dynamic_slice_in_dim(group_states[0], jnp.maximum(first_segment - 1, 0), 1) * (
            position > 0
        ).astype(jnp.float32)
        after = lax.dynamic_slice_in_dim(
            group_states[0], jnp.minimum(first_segment + seg_dev, group_length - 1), 1
        ) * (position < members - 1).astype(jnp.float32)
        left_values = jnp.concatenate([before, frac_pressure[:-1]])
        right_values = jnp.concatenate([frac_pressure[1:], after])
        cell_pressure = pressure.reshape(-1)[cell_flat]
        cell_saturation = saturation.reshape(-1)[cell_flat]
        upwind_now = upwind_all[outer].reshape(-1)
        upwind_sat = jnp.where(upwind_now == 1, cell_saturation, seg_saturation)
        weight = jnp.where(
            live_slots == 1, transmit * (MOBILITY_FLOOR + upwind_sat * upwind_sat), jnp.float32(0.0)
        )
        water_flux = weight * (cell_pressure - seg_pressure) * upwind_sat
        cell_terms = jnp.stack([weight, weight * seg_pressure, water_flux])
        cell_totals = (
            jnp.zeros((3, row_count * column_count), jnp.float32).at[:, cell_flat].add(cell_terms)
        )
        couple = cell_totals[0].reshape(row_count, column_count)
        source_term = cell_totals[1].reshape(row_count, column_count)
        water_lost = cell_totals[2].reshape(row_count, column_count)
        owner_terms = jnp.stack([weight * cell_pressure, weight, water_flux])
        arrived = lax.all_to_all(
            owner_terms.reshape(3, members, capacity),
            "frac",
            split_axis=1,
            concat_axis=1,
            tiled=True,
        )
        segment_totals = (
            jnp.zeros((3, seg_dev), jnp.float32)
            .at[:, targets.reshape(-1)]
            .add(arrived.reshape(3, -1))
        )
        diagonal = 4.0 + matrix_perm + couple
        right_side = matrix_perm * pressure + source_term
        new_pressure = chebyshev(pressure, right_side, diagonal)
        new_saturation = saturation - TAU_STEP * water_lost / (matrix_perm + couple)
        inflow = segment_totals[0]
        weight_total = segment_totals[1]
        gained = segment_totals[2]
        new_frac_pressure = (aperture * frac_pressure + inflow + left_values + right_values) / (
            aperture + weight_total + 2.0
        )
        new_frac_saturation = frac_saturation + TAU_STEP * gained / (aperture + weight_total)
        pressure = new_pressure
        saturation = new_saturation
        frac_pressure = new_frac_pressure
        frac_saturation = new_frac_saturation
    matrix_out = jnp.stack([pressure, saturation])
    frac_out = jnp.stack([frac_pressure, frac_saturation])[:, None, :]
    return (matrix_out, frac_out)


def solution(mesh):
    return jax.shard_map(
        on_device,
        mesh=mesh,
        in_specs=(
            P(None, "grp", "frac"),
            P("grp", "frac"),
            P(None, "grp", "frac"),
            P("grp", "frac"),
            P("grp", "frac", None, None),
            P("grp", "frac", None, None),
            P("grp", "frac", None, None),
            P("grp", "frac", None),
            P(None, "grp", "frac", None, None),
        ),
        out_specs=(P(None, "grp", "frac"), P(None, "grp", "frac")),
        check_vma=False,
    )
```

profile of v0, /device:TPU:1, one launch (start us, length us, event | category | flops | bytes accessed | tf_op | source)
XLA Modules:
  0.0 877.5 jit_solution(15315427686582233729)
XLA Ops:
  7.9 4.9 collective-permute-start.1
  16.1 6.8 all-to-all-start
  31.0 23.0 %gather_fusion.3 = f32[4096]{0:T(1024)S(1)} fusion(f32[32768]{0:T(1024)S(1)} %bitcast.174, s32[4096]{0:T(1024)S(1)} %broadcast_clamp_fusion.1), kind=kCustom, calls=%fused_computation.3 | custom fusion | bytes 49152 | tf_op jit(solution)/shard_map/gather | solution.py:115
  54.2 23.0 %gather_fusion = f32[4096]{0:T(1024)S(1)} fusion(f32[32768]{0:T(1024)S(1)} %bitcast.175, s32[4096]{0:T(1024)S(1)} %broadcast_clamp_fusion.1), kind=kCustom, calls=%fused_computation | custom fusion | bytes 49152 | tf_op jit(solution)/shard_map/gather | solution.py:116
  79.3 4.6 collective-permute-start.3
  86.3 23.0 %gather_fusion.1 = f32[4096]{0:T(1024)S(1)} fusion(f32[131072]{0:T(1024)S(1)} %bitcast.183, s32[4096]{0:T(1024)S(1)} %broadcast_clamp_fusion), kind=kCustom, calls=%fused_computation.1 | custom fusion | bytes 49152 | tf_op jit(solution)/shard_map/gather | solution.py:104
  109.4 23.0 %gather_fusion.2 = f32[4096]{0:T(1024)S(1)} fusion(f32[131072]{0:T(1024)S(1)} %bitcast.181, s32[4096]{0:T(1024)S(1)} %broadcast_clamp_fusion), kind=kCustom, calls=%fused_computation.2 | custom fusion | bytes 49152 | tf_op jit(solution)/shard_map/gather | solution.py:103
  134.9 29.4 %scatter_custom_fusion = f32[3,32768]{0,1:T(8,128)} fusion(s32[4096]{0:T(1024)S(1)} %bitcast.233, f32[4096,3]{1,0:T(8,128)S(1)} %copy.114, f32[]{:T(128)} %constant.24.clone.1), kind=kCustom, calls=%fused_computation.34 | custom fusion | flops 12288 | bytes 393220 | tf_op jit(solution)/shard_map/scatter-add | solution.py:125
  164.4 30.7 %slice_reduce_fusion.4 = (f32[32768]{0:T(1024)S(1)}, f32[32768]{0:T(1024)S(1)}, f32[32768]{0:T(1024)S(1)}) fusion(f32[3,32768]{0,1:T(8,128)} %scatter_custom_fusion), kind=kLoop, calls=%fused_computation.28 | loop fusion | flops 32768 | bytes 786432 | tf_op jit(solution)/shard_map/slice | solution.py:128
  197.0 4.5 collective-permute-start.5
  207.8 4.0 collective-permute-start.7
  220.0 11.2 %all-to-all-start.1 = ((f32[3,16,256]{2,0,1:T(4,128)}), f32[3,16,256]{2,0,1:T(4,128)S(1)}, u32[]{:S(2)}, u32[]{:S(2)}) async-start(f32[3,16,256]{2,0,1:T(4,128)} %copy.115), calls=%async_computation.1 | async-start | bytes 131072 | tf_op jit(solution)/shard_map/all_to_all | solution.py:131
  235.1 4.0 collective-permute-start.11
  239.8 25.0 %scatter_custom_fusion.1 = f32[3,8192]{0,1:T(8,128)} fusion(s32[4096]{0:T(1024)S(1)} %bitcast.240, f32[4096,3]{1,0:T(8,128)S(1)} %copy.116, f32[]{:T(128)} %constant.24.clone.1), kind=kCustom, calls=%fused_computation.40 | custom fusion | flops 12288 | bytes 98308 | tf_op jit(solution)/shard_map/scatter-add | solution.py:141
  264.8 11.9 %fusion.150 = (f32[1,8192]{0,1:T(8,128)}, f32[1,8192]{0,1:T(8,128)}, f32[1,8192]{0,1:T(8,128)}) fusion(f32[3,8192]{0,1:T(8,128)} %scatter_custom_fusion.1), kind=kLoop, calls=%fused_computation.351 | loop fusion | bytes 196608 | tf_op jit(solution)/shard_map/slice | solution.py:147
  288.0 4.5 collective-permute-start.13
  298.8 4.2 collective-permute-start.15
  309.4 23.0 %gather_fusion.4 = f32[4096]{0:T(1024)S(1)} fusion(f32[32768]{0:T(1024)S(1)} %bitcast.178, s32[4096]{0:T(1024)S(1)} %broadcast_clamp_fusion.1), kind=kCustom, calls=%fused_computation.4 | custom fusion | bytes 49152 | tf_op jit(solution)/shard_map/gather | solution.py:116
  332.6 23.0 %gather_fusion.7 = f32[4096]{0:T(1024)S(1)} fusion(f32[32768]{0:T(1024)S(1)} %bitcast.179, s32[4096]{0:T(1024)S(1)} %broadcast_clamp_fusion.1), kind=kCustom, calls=%fused_computation.7 | custom fusion | bytes 49152 | tf_op jit(solution)/shard_map/gather | solution.py:115
  357.7 5.3 collective-permute-start.19
  366.2 23.0 %gather_fusion.5 = f32[4096]{0:T(1024)S(1)} fusion(f32[131072]{0:T(1024)S(1)} %bitcast.184, s32[4096]{0:T(1024)S(1)} %broadcast_clamp_fusion), kind=kCustom, calls=%fused_computation.5 | custom fusion | bytes 49152 | tf_op jit(solution)/shard_map/gather | solution.py:104
  389.3 23.0 %gather_fusion.6 = f32[4096]{0:T(1024)S(1)} fusion(f32[131072]{0:T(1024)S(1)} %bitcast.182, s32[4096]{0:T(1024)S(1)} %broadcast_clamp_fusion), kind=kCustom, calls=%fused_computation.6 | custom fusion | bytes 49152 | tf_op jit(solution)/shard_map/gather | solution.py:103
  415.1 29.5 %scatter_custom_fusion.2 = f32[3,32768]{0,1:T(8,128)} fusion(s32[4096]{0:T(1024)} %bitcast.234, f32[4096,3]{1,0:T(8,128)S(1)} %copy.120, f32[]{:T(128)} %constant.24.clone.1), kind=kCustom, calls=%fused_computation.32 | custom fusion | flops 12288 | bytes 393728 | tf_op jit(solution)/shard_map/scatter-add | solution.py:125
  444.7 30.7 %slice_reduce_fusion.2 = (f32[32768]{0:T(1024)S(1)}, f32[32768]{0:T(1024)S(1)}, f32[32768]{0:T(1024)S(1)}) fusion(f32[3,32768]{0,1:T(8,128)} %scatter_custom_fusion.2), kind=kLoop, calls=%fused_computation.24 | loop fusion | flops 32768 | bytes 786432 | tf_op jit(solution)/shard_map/slice | solution.py:128
  476.7 3.9 collective-permute-start.21
  486.9 4.0 collective-permute-start.23
  493.4 14.7 %all-to-all-start.2 = ((f32[3,16,256]{2,0,1:T(4,128)}), f32[3,16,256]{2,0,1:T(4,128)S(1)}, u32[]{:S(2)}, u32[]{:S(2)}) async-start(f32[3,16,256]{2,0,1:T(4,128)} %copy.121), calls=%async_computation.2 | async-start | bytes 131072 | tf_op jit(solution)/shard_map/all_to_all | solution.py:131
  509.4 3.4 collective-permute-start.25
  515.3 24.9 %scatter_custom_fusion.3 = f32[3,8192]{0,1:T(8,128)} fusion(s32[4096]{0:T(1024)} %bitcast.241, f32[4096,3]{1,0:T(8,128)S(1)} %copy.122, f32[]{:T(128)} %constant.24.clone.1), kind=kCustom, calls=%fused_computation.38 | custom fusion | flops 12288 | bytes 98816 | tf_op jit(solution)/shard_map/scatter-add | solution.py:141
  540.3 11.9 %fusion.149 = (f32[1,8192]{0,1:T(8,128)}, f32[1,8192]{0,1:T(8,128)}, f32[1,8192]{0,1:T(8,128)}) fusion(f32[3,8192]{0,1:T(8,128)} %scatter_custom_fusion.3), kind=kLoop, calls=%fused_computation.350 | loop fusion | bytes 196608 | tf_op jit(solution)/shard_map/slice | solution.py:147
  563.2 4.2 collective-permute-start.27
  569.0 5.5 collective-permute-start.29
  580.7 5.0 collective-permute-start.31
  591.7 23.0 %gather_fusion.8 = f32[4096]{0:T(1024)S(1)} fusion(f32[32768]{0:T(1024)S(1)} %bitcast.176, s32[4096]{0:T(1024)S(1)} %copy-done.10), kind=kCustom, calls=%fused_computation.8 | custom fusion | bytes 49152 | tf_op jit(solution)/shard_map/gather | solution.py:116
  614.9 23.0 %gather_fusion.11 = f32[4096]{0:T(1024)S(1)} fusion(f32[32768]{0:T(1024)S(1)} %bitcast.177, s32[4096]{0:T(1024)S(1)} %copy-done.10), kind=kCustom, calls=%fused_computation.11 | custom fusion | bytes 49152 | tf_op jit(solution)/shard_map/gather | solution.py:115
  640.0 5.3 collective-permute-start.35
  647.7 23.0 %gather_fusion.9 = f32[4096]{0:T(1024)S(1)} fusion(f32[131072]{0:T(1024)S(1)} %bitcast.185, s32[4096]{0:T(1024)S(1)} %broadcast_clamp_fusion), kind=kCustom, calls=%fused_computation.9 | custom fusion | bytes 49152 | tf_op jit(solution)/shard_map/gather | solution.py:104
  670.8 23.0 %gather_fusion.10 = f32[4096]{0:T(1024)S(1)} fusion(f32[131072]{0:T(1024)S(1)} %bitcast.180, s32[4096]{0:T(1024)S(1)} %broadcast_clamp_fusion), kind=kCustom, calls=%fused_computation.10 | custom fusion | bytes 49152 | tf_op jit(solution)/shard_map/gather | solution.py:103
  696.7 29.6 %scatter_custom_fusion.4 = f32[3,32768]{0,1:T(8,128)} fusion(s32[4096]{0:T(1024)} %bitcast.235, f32[4096,3]{1,0:T(8,128)S(1)} %copy.126, f32[]{:T(128)} %constant.24.clone.1), kind=kCustom, calls=%fused_computation.30 | custom fusion | flops 12288 | bytes 393728 | tf_op jit(solution)/shard_map/scatter-add | solution.py:125
  726.4 30.7 %slice_reduce_fusion = (f32[32768]{0:T(1024)S(1)}, f32[32768]{0:T(1024)S(1)}, f32[32768]{0:T(1024)S(1)}) fusion(f32[3,32768]{0,1:T(8,128)} %scatter_custom_fusion.4), kind=kLoop, calls=%fused_computation.20 | loop fusion | flops 32768 | bytes 786432 | tf_op jit(solution)/shard_map/slice | solution.py:128
  758.4 3.9 collective-permute-start.37
  768.6 4.0 collective-permute-start.39
  775.2 3.4 collective-permute-start.41
  784.8 5.4 collective-permute-start.43
  799.1 16.2 %all-to-all-start.3 = ((f32[3,16,256]{2,0,1:T(4,128)}), f32[3,16,256]{2,0,1:T(4,128)S(1)}, u32[]{:S(2)}, u32[]{:S(2)}) async-start(f32[3,16,256]{2,0,1:T(4,128)} %copy.127), calls=%async_computation.3 | async-start | bytes 131072 | tf_op jit(solution)/shard_map/all_to_all | solution.py:131
  816.8 4.0 collective-permute-start.47
  824.0 25.0 %scatter_custom_fusion.5 = f32[3,8192]{0,1:T(8,128)} fusion(s32[4096]{0:T(1024)} %bitcast.242, f32[4096,3]{1,0:T(8,128)S(1)} %copy.128, f32[]{:T(128)} %constant.24.clone.1), kind=kCustom, calls=%fused_computation.36 | custom fusion | flops 12288 | bytes 98816 | tf_op jit(solution)/shard_map/scatter-add | solution.py:141
  849.1 11.9 %fusion.148 = (f32[1,8192]{0,1:T(8,128)}, f32[1,8192]{0,1:T(8,128)}, f32[1,8192]{0,1:T(8,128)}) fusion(f32[3,8192]{0,1:T(8,128)} %scatter_custom_fusion.5), kind=kLoop, calls=%fused_computation.349 | loop fusion | bytes 196608 | tf_op jit(solution)/shard_map/slice | solution.py:147
  (430 shorter events, 152.4 us)
Async XLA Ops:
  7.9 69.3 %collective-permute-start.1 = (f32[1,256]{1,0:T(1,128)S(1)}, f32[1,256]{1,0:T(1,128)S(1)}, u32[]{:S(2)}, u32[]{:S(2)}) collective-permute-start(f32[1,256]{1,0:T(1,128)S(1)} %get-tuple-element.83), channel_id=1, source_target_pairs={{0,16},{16,32},{32,48},{48,64},{64,80},{80,96},{96,112},{1,17},{17... | collective-permute-start | bytes 3080 | tf_op jit(solution)/shard_map/ppermute | solution.py:24
  12.8 64.4 %collective-permute-start = (f32[1,256]{1,0:T(1,128)S(1)}, f32[1,256]{1,0:T(1,128)S(1)}, u32[]{:S(2)}, u32[]{:S(2)}) collective-permute-start(f32[1,256]{1,0:T(1,128)S(1)} %get-tuple-element.84), channel_id=1, source_target_pairs={{16,0},{32,16},{48,32},{64,48},{80,64},{96,80},{112,96},{17,1},{33... | collective-permute-start | bytes 3080 | tf_op jit(solution)/shard_map/ppermute | solution.py:26
  16.1 187.3 %all-to-all-start = ((s32[16,1,256]{2,1,0:T(1,128)}), s32[16,1,256]{2,1,0:T(1,128)}, u32[]{:S(2)}, u32[]{:S(2)}) async-start(s32[16,1,256]{2,1,0:T(1,128)} %all_to_all.15), calls=%async_computation | async-start | bytes 32768 | tf_op jit(solution)/shard_map/all_to_all | solution.py:59
  22.9 61.0 %all-gather.4.cloned.1.call-start = ((), (), s32[]{:S(2)}) async-start(), calls=%async_computation.4 | async-start | bytes 1114112 | tf_op jit(solution)/shard_map/all_gather | solution.py:100
  78.0 117.2 %collective-permute-start.2 = (f32[130,1]{1,0:T(8,128)}, f32[130,1]{1,0:T(8,128)S(1)}, u32[]{:S(2)}, u32[]{:S(2)}) collective-permute-start(f32[130,1]{1,0:T(8,128)} %get-tuple-element.110), channel_id=1, source_target_pairs={{1,0},{2,1},{3,2},{4,3},{5,4},{6,5},{7,6},{8,7},{9,8},{10,9},{11,1... | collective-permute-start | bytes 1568 | tf_op jit(solution)/shard_map/ppermute | solution.py:26
  79.3 116.6 %collective-permute-start.3 = (f32[130,1]{1,0:T(8,128)}, f32[130,1]{1,0:T(8,128)}, u32[]{:S(2)}, u32[]{:S(2)}) collective-permute-start(f32[130,1]{1,0:T(8,128)} %get-tuple-element.111), channel_id=1, source_target_pairs={{0,1},{1,2},{2,3},{3,4},{4,5},{5,6},{6,7},{7,8},{8,9},{9,10},{10,1... | collective-permute-start | bytes 1568 | tf_op jit(solution)/shard_map/ppermute | solution.py:24
  197.0 7.2 collective-permute-start.5
  206.5 5.4 collective-permute-start.6
  214.3 18.8 %collective-permute-start.9 = (f32[1,256]{1,0:T(1,128)S(1)}, f32[1,256]{1,0:T(1,128)S(1)}, u32[]{:S(2)}, u32[]{:S(2)}) collective-permute-start(f32[1,256]{1,0:T(1,128)S(1)} %get-tuple-element.132), channel_id=1, source_target_pairs={{0,16},{16,32},{32,48},{48,64},{64,80},{80,96},{96,112},{1,17},{17... | collective-permute-start | bytes 3080 | tf_op jit(solution)/shard_map/ppermute | solution.py:24
  217.4 15.7 %collective-permute-start.8 = (f32[1,256]{1,0:T(1,128)S(1)}, f32[1,256]{1,0:T(1,128)S(1)}, u32[]{:S(2)}, u32[]{:S(2)}) collective-permute-start(f32[1,256]{1,0:T(1,128)S(1)} %get-tuple-element.133), channel_id=1, source_target_pairs={{16,0},{32,16},{48,32},{64,48},{80,64},{96,80},{112,96},{17,1},{33... | collective-permute-start | bytes 3080 | tf_op jit(solution)/shard_map/ppermute | solution.py:26
  220.0 19.1 %all-to-all-start.1 = ((f32[3,16,256]{2,0,1:T(4,128)}), f32[3,16,256]{2,0,1:T(4,128)S(1)}, u32[]{:S(2)}, u32[]{:S(2)}) async-start(f32[3,16,256]{2,0,1:T(4,128)} %copy.115), calls=%async_computation.1 | async-start | bytes 131072 | tf_op jit(solution)/shard_map/all_to_all | solution.py:131
  231.2 132.6 %all-gather.6.cloned.1.call-start = ((), (), s32[]{:S(2)}) async-start(), calls=%async_computation.5 | async-start | bytes 1114112 | tf_op jit(solution)/shard_map/all_gather | solution.py:100
  233.8 52.4 %collective-permute-start.10 = (f32[130,1]{1,0:T(8,128)}, f32[130,1]{1,0:T(8,128)S(1)}, u32[]{:S(2)}, u32[]{:S(2)}) collective-permute-start(f32[130,1]{1,0:T(8,128)} %get-tuple-element.106), channel_id=1, source_target_pairs={{1,0},{2,1},{3,2},{4,3},{5,4},{6,5},{7,6},{8,7},{9,8},{10,9},{11,1... | collective-permute-start | bytes 1568 | tf_op jit(solution)/shard_map/ppermute | solution.py:26
  235.1 51.1 %collective-permute-start.11 = (f32[130,1]{1,0:T(8,128)}, f32[130,1]{1,0:T(8,128)S(1)}, u32[]{:S(2)}, u32[]{:S(2)}) collective-permute-start(f32[130,1]{1,0:T(8,128)} %get-tuple-element.107), channel_id=1, source_target_pairs={{0,1},{1,2},{2,3},{3,4},{4,5},{5,6},{6,7},{7,8},{8,9},{9,10},{10,1... | collective-permute-start | bytes 1568 | tf_op jit(solution)/shard_map/ppermute | solution.py:24
  288.0 6.4 collective-permute-start.13
  297.5 5.5 collective-permute-start.14
  298.8 5.5 collective-permute-start.15
  304.5 51.2 %collective-permute-start.17 = (f32[1,256]{1,0:T(1,128)S(1)}, f32[1,256]{1,0:T(1,128)S(1)}, u32[]{:S(2)}, u32[]{:S(2)}) collective-permute-start(f32[1,256]{1,0:T(1,128)S(1)} %get-tuple-element.126), channel_id=1, source_target_pairs={{0,16},{16,32},{32,48},{48,64},{64,80},{80,96},{96,112},{1,17},{17... | collective-permute-start | bytes 3080 | tf_op jit(solution)/shard_map/ppermute | solution.py:24
  307.4 48.3 %collective-permute-start.16 = (f32[1,256]{1,0:T(1,128)S(1)}, f32[1,256]{1,0:T(1,128)S(1)}, u32[]{:S(2)}, u32[]{:S(2)}) collective-permute-start(f32[1,256]{1,0:T(1,128)S(1)} %get-tuple-element.127), channel_id=1, source_target_pairs={{16,0},{32,16},{48,32},{64,48},{80,64},{96,80},{112,96},{17,1},{33... | collective-permute-start | bytes 3080 | tf_op jit(solution)/shard_map/ppermute | solution.py:26
  356.4 119.1 %collective-permute-start.18 = (f32[130,1]{1,0:T(8,128)}, f32[130,1]{1,0:T(8,128)}, u32[]{:S(2)}, u32[]{:S(2)}) collective-permute-start(f32[130,1]{1,0:T(8,128)} %get-tuple-element.102), channel_id=1, source_target_pairs={{1,0},{2,1},{3,2},{4,3},{5,4},{6,5},{7,6},{8,7},{9,8},{10,9},{11,1... | collective-permute-start | bytes 1568 | tf_op jit(solution)/shard_map/ppermute | solution.py:26
  357.7 117.9 %collective-permute-start.19 = (f32[130,1]{1,0:T(8,128)}, f32[130,1]{1,0:T(8,128)}, u32[]{:S(2)}, u32[]{:S(2)}) collective-permute-start(f32[130,1]{1,0:T(8,128)} %get-tuple-element.103), channel_id=1, source_target_pairs={{0,1},{1,2},{2,3},{3,4},{4,5},{5,6},{6,7},{7,8},{8,9},{9,10},{10,1... | collective-permute-start | bytes 1568 | tf_op jit(solution)/shard_map/ppermute | solution.py:24
  476.7 6.0 collective-permute-start.21
  485.6 22.5 %collective-permute-start.22 = (f32[130,1]{1,0:T(8,128)S(1)}, f32[130,1]{1,0:T(8,128)S(1)}, u32[]{:S(2)}, u32[]{:S(2)}) collective-permute-start(f32[130,1]{1,0:T(8,128)S(1)} %get-tuple-element.100), channel_id=1, source_target_pairs={{1,0},{2,1},{3,2},{4,3},{5,4},{6,5},{7,6},{8,7},{9,8},{10,9},{11,1... | collective-permute-start | bytes 1568 | tf_op jit(solution)/shard_map/ppermute | solution.py:26
  486.9 21.2 %collective-permute-start.23 = (f32[130,1]{1,0:T(8,128)S(1)}, f32[130,1]{1,0:T(8,128)S(1)}, u32[]{:S(2)}, u32[]{:S(2)}) collective-permute-start(f32[130,1]{1,0:T(8,128)S(1)} %get-tuple-element.101), channel_id=1, source_target_pairs={{0,1},{1,2},{2,3},{3,4},{4,5},{5,6},{6,7},{7,8},{8,9},{9,10},{10,1... | collective-permute-start | bytes 1568 | tf_op jit(solution)/shard_map/ppermute | solution.py:24
  493.4 21.2 %all-to-all-start.2 = ((f32[3,16,256]{2,0,1:T(4,128)}), f32[3,16,256]{2,0,1:T(4,128)S(1)}, u32[]{:S(2)}, u32[]{:S(2)}) async-start(f32[3,16,256]{2,0,1:T(4,128)} %copy.121), calls=%async_computation.2 | async-start | bytes 131072 | tf_op jit(solution)/shard_map/all_to_all | solution.py:131
  508.1 137.1 %all-gather.8.cloned.1.call-start = ((), (), s32[]{:S(2)}) async-start(), calls=%async_computation.6 | async-start | bytes 1114112 | tf_op jit(solution)/shard_map/all_gather | solution.py:100
  509.4 52.4 %collective-permute-start.25 = (f32[1,256]{1,0:T(1,128)S(1)}, f32[1,256]{1,0:T(1,128)S(1)}, u32[]{:S(2)}, u32[]{:S(2)}) collective-permute-start(f32[1,256]{1,0:T(1,128)S(1)} %get-tuple-element.122), channel_id=1, source_target_pairs={{0,16},{16,32},{32,48},{48,64},{64,80},{80,96},{96,112},{1,17},{17... | collective-permute-start | bytes 3080 | tf_op jit(solution)/shard_map/ppermute | solution.py:24
  512.7 49.1 %collective-permute-start.24 = (f32[1,256]{1,0:T(1,128)S(1)}, f32[1,256]{1,0:T(1,128)S(1)}, u32[]{:S(2)}, u32[]{:S(2)}) collective-permute-start(f32[1,256]{1,0:T(1,128)S(1)} %get-tuple-element.123), channel_id=1, source_target_pairs={{16,0},{32,16},{48,32},{64,48},{80,64},{96,80},{112,96},{17,1},{33... | collective-permute-start | bytes 3080 | tf_op jit(solution)/shard_map/ppermute | solution.py:26
  561.9 5.9 collective-permute-start.26
  563.2 5.5 collective-permute-start.27
  569.0 7.4 collective-permute-start.29
  579.4 6.6 collective-permute-start.30
  580.7 6.4 collective-permute-start.31
  587.3 50.6 %collective-permute-start.33 = (f32[1,256]{1,0:T(1,128)S(1)}, f32[1,256]{1,0:T(1,128)S(1)}, u32[]{:S(2)}, u32[]{:S(2)}) collective-permute-start(f32[1,256]{1,0:T(1,128)S(1)} %get-tuple-element.118), channel_id=1, source_target_pairs={{0,16},{16,32},{32,48},{48,64},{64,80},{80,96},{96,112},{1,17},{17... | collective-permute-start | bytes 3080 | tf_op jit(solution)/shard_map/ppermute | solution.py:24
  589.7 48.2 %collective-permute-start.32 = (f32[1,256]{1,0:T(1,128)S(1)}, f32[1,256]{1,0:T(1,128)S(1)}, u32[]{:S(2)}, u32[]{:S(2)}) collective-permute-start(f32[1,256]{1,0:T(1,128)S(1)} %get-tuple-element.119), channel_id=1, source_target_pairs={{16,0},{32,16},{48,32},{64,48},{80,64},{96,80},{112,96},{17,1},{33... | collective-permute-start | bytes 3080 | tf_op jit(solution)/shard_map/ppermute | solution.py:26
  638.7 118.6 %collective-permute-start.34 = (f32[130,1]{1,0:T(8,128)}, f32[130,1]{1,0:T(8,128)}, u32[]{:S(2)}, u32[]{:S(2)}) collective-permute-start(f32[130,1]{1,0:T(8,128)} %get-tuple-element.94), channel_id=1, source_target_pairs={{1,0},{2,1},{3,2},{4,3},{5,4},{6,5},{7,6},{8,7},{9,8},{10,9},{11,1... | collective-permute-start | bytes 1568 | tf_op jit(solution)/shard_map/ppermute | solution.py:26
  640.0 117.3 %collective-permute-start.35 = (f32[130,1]{1,0:T(8,128)}, f32[130,1]{1,0:T(8,128)}, u32[]{:S(2)}, u32[]{:S(2)}) collective-permute-start(f32[130,1]{1,0:T(8,128)} %get-tuple-element.95), channel_id=1, source_target_pairs={{0,1},{1,2},{2,3},{3,4},{4,5},{5,6},{6,7},{7,8},{8,9},{9,10},{10,1... | collective-permute-start | bytes 1568 | tf_op jit(solution)/shard_map/ppermute | solution.py:24
  758.4 5.9 collective-permute-start.37
  767.3 5.4 collective-permute-start.38
  768.6 5.3 collective-permute-start.39
  775.2 5.4 collective-permute-start.41
  783.5 6.7 collective-permute-start.42
  784.8 6.7 collective-permute-start.43
  791.7 23.6 %collective-permute-start.45 = (f32[1,256]{1,0:T(1,128)S(1)}, f32[1,256]{1,0:T(1,128)S(1)}, u32[]{:S(2)}, u32[]{:S(2)}) collective-permute-start(f32[1,256]{1,0:T(1,128)S(1)} %get-tuple-element.112), channel_id=1, source_target_pairs={{0,16},{16,32},{32,48},{48,64},{64,80},{80,96},{96,112},{1,17},{17... | collective-permute-start | bytes 3080 | tf_op jit(solution)/shard_map/ppermute | solution.py:24
  794.6 20.8 %collective-permute-start.44 = (f32[1,256]{1,0:T(1,128)S(1)}, f32[1,256]{1,0:T(1,128)S(1)}, u32[]{:S(2)}, u32[]{:S(2)}) collective-permute-start(f32[1,256]{1,0:T(1,128)S(1)} %get-tuple-element.113), channel_id=1, source_target_pairs={{16,0},{32,16},{48,32},{64,48},{80,64},{96,80},{112,96},{17,1},{33... | collective-permute-start | bytes 3080 | tf_op jit(solution)/shard_map/ppermute | solution.py:26
  799.1 24.3 %all-to-all-start.3 = ((f32[3,16,256]{2,0,1:T(4,128)}), f32[3,16,256]{2,0,1:T(4,128)S(1)}, u32[]{:S(2)}, u32[]{:S(2)}) async-start(f32[3,16,256]{2,0,1:T(4,128)} %copy.127), calls=%async_computation.3 | async-start | bytes 131072 | tf_op jit(solution)/shard_map/all_to_all | solution.py:131
  815.5 5.5 collective-permute-start.46
  816.8 5.7 collective-permute-start.47
  (102 other events, 3319.0 us)
Sparse Core Ops, SparseCore 0:
  26.4 43.4 all-gather.3
  286.4 46.0 all-gather.5
  561.9 43.4 all-gather.7
where the time goes:
time: 893 us; the launch traced here: 877 us
  local copies, waits for them, and re-layouts  370 us (41%)
  other arithmetic  274 us (31%)
  starting transfers between devices  186 us (21%)
  waiting for transfers between devices  26.2 us (3%)
  between operations  20.9 us (2%)
    ppermute x24, starting transfers between devices, extended(): lax.ppermute(tail, axis, [(i, (i + 1) % count) for i in range(ends)])  99 us
    slice x3, other arithmetic, on_device(): source_term = cell_totals[1].reshape(row_count, column_count)  92 us
    scatter-add x3, other arithmetic, on_device(): jnp.zeros((3, row_count * column_count), jnp.float32).at[:, cell_flat]  88.5 us
    scatter-add x3, other arithmetic, on_device(): segment_totals = jnp.zeros((3, seg_dev), jnp.float32).at[:, targets.resha...  75 us
    gather x6, local copies, waits for them, and re-layouts, on_device(): cell_pressure = pressure.reshape(-1)[cell_flat]  69.1 us
    gather x6, local copies, waits for them, and re-layouts, on_device(): seg_saturation = group_states[1][global_segment]  69.1 us
    gather x6, local copies, waits for them, and re-layouts, on_device(): cell_saturation = saturation.reshape(-1)[cell_flat]  69.1 us
    gather x6, local copies, waits for them, and re-layouts, on_device(): seg_pressure = group_states[0][global_segment]  69.1 us
  transfers between devices with their start and end apart: 55, of which 16 were waited for; matrix products, arithmetic and copies ran while one was open for 67% of the time, Pallas kernels for 0%

commit v1 on v0

v1 whole, which is shorter than its diff:
```python
import functools

import jax
import jax.numpy as jnp
from jax import lax
from jax.experimental import pallas as pl
from jax.experimental.pallas import tpu as pltpu
from jax.sharding import PartitionSpec as P

ITERS = 3
SWEEPS = 4
LOW_BOUND = 0.02
HIGH_BOUND = 1.98
TAU_STEP = 0.5
MOBILITY_FLOOR = 0.2

F32 = jnp.float32
BF16 = jnp.bfloat16
MESH = pl.DeviceIdType.MESH
LANES = 128
ROWS = 8
AROUND = ((-1, 0), (1, 0), (0, -1), (0, 1), (-1, -1), (-1, 1), (1, -1), (1, 1))


def pieces(value):
    high = value.astype(BF16)
    low = (value - high.astype(F32)).astype(BF16)
    return high, low


def one_hot(index, count):
    ids = lax.broadcasted_iota(jnp.int32, (count, index.shape[1]), 0)
    return jnp.where(ids == index, F32(1.0), F32(0.0)).astype(BF16)


def spread(hot, values):
    rows, count = hot.shape
    stacked = hot.reshape(rows // 16, 16, count)
    out = []
    for value in values:
        for part in pieces(jnp.broadcast_to(value, (16, count))):
            out.append((stacked * part[None]).reshape(rows, count))
    return jnp.concatenate(out, axis=0)


def flux_terms(trans, upwind, cell_p, cell_s, seg_p, seg_s):
    u = jnp.where(upwind > 0.5, cell_s, seg_s)
    weight = trans * (MOBILITY_FLOOR + u * u)
    return weight, weight * (cell_p - seg_p) * u


def kernel(
    groups,
    members,
    cap,
    state_ref,
    perm_ref,
    frac_ref,
    aperture_ref,
    cell_ref,
    seg_ref,
    trans_ref,
    count_ref,
    upwind_ref,
    matrix_out,
    frac_out,
    stat_send,
    stat_recv,
    p_send,
    p_recv,
    f_send,
    f_recv,
    edge_left,
    edge_right,
    fields,
    sat,
    fq,
    side_send,
    halo_row,
    halo_col,
    col_hot,
    row_hot,
    low_hot,
    high_hot,
    cell_acc,
    seg_acc,
    ext_x,
    ext_inv,
    ext_c,
    stat_ss,
    stat_rs,
    p_ss,
    p_rs,
    f_ss,
    f_rs,
    edge_ss,
    edge_rs,
    halo_ss,
    halo_rs,
):
    g = lax.axis_index("grp")
    me = lax.axis_index("frac")
    slots = members * cap
    rows, cols = perm_ref.shape
    seg_rows = aperture_ref.shape[0]
    group = min(slots, 4 * cap)

    def member(step):
        return lax.rem(me + step + members, members)

    def neighbour(step):
        return (lax.rem(g + step[0] + groups, groups), member(step[1]))

    barrier = pltpu.get_barrier_semaphore()
    for k in range(1, members):
        pl.semaphore_signal(barrier, inc=1, device_id=(g, member(k)), device_id_type=MESH)
    apart = [step for step in AROUND if step[0] != 0]
    for step in apart:
        pl.semaphore_signal(barrier, inc=1, device_id=neighbour(step), device_id_type=MESH)

    def lanes(block, width):
        return pl.ds(pl.multiple_of(block * width, width), width)

    eye = lax.broadcasted_iota(jnp.int32, (members, members), 0) == lax.broadcasted_iota(
        jnp.int32, (members, members), 1
    )
    counts = jnp.sum(
        jnp.where(eye, jnp.broadcast_to(count_ref[...].astype(F32), (members, members)), 0.0),
        axis=1,
        keepdims=True,
    )
    place = lax.broadcasted_iota(jnp.int32, (members, cap), 1).astype(F32)
    live_trans = jnp.where(place < counts, trans_ref[...], F32(0.0))
    seg_float = seg_ref[...].astype(F32)
    ups = [upwind_ref[t].astype(F32) for t in range(ITERS)]
    stat_send[...] = jnp.zeros_like(stat_send)
    for o in range(members):
        here = slice(o * cap, (o + 1) * cap)
        stat_send[0:1, here] = live_trans[o : o + 1, :]
        stat_send[1:2, here] = seg_float[o : o + 1, :]
        for t in range(ITERS):
            stat_send[2 + t : 3 + t, here] = ups[t][o : o + 1, :]

    pl.semaphore_wait(barrier, members - 1 + len(apart))

    def exchange(send, recv, send_sem, recv_sem, k):
        to = member(k)
        return pltpu.make_async_remote_copy(
            src_ref=send.at[:, lanes(to, cap)],
            dst_ref=recv.at[:, lanes(me, cap)],
            send_sem=send_sem,
            recv_sem=recv_sem,
            device_id=(g, to),
            device_id_type=MESH,
        )

    def stat_copy(k):
        return exchange(stat_send, stat_recv, stat_ss.at[k], stat_rs.at[k], k)

    def p_copy(t, k):
        return exchange(p_send.at[t], p_recv.at[t], p_ss.at[t, k], p_rs.at[t, k], k)

    def f_copy(t, k):
        return exchange(f_send.at[t], f_recv.at[t], f_ss.at[t, k], f_rs.at[t, k], k)

    def each(body):
        lax.fori_loop(1, members, lambda k, c: (body(k), c)[1], 0)

    each(lambda k: stat_copy(k).start())
    stat_recv[:, lanes(me, cap)] = stat_send[:, lanes(me, cap)]

    def edge_copies(t):
        return (
            pltpu.make_async_remote_copy(
                src_ref=fq.at[t, 0, pl.ds(seg_rows - ROWS, ROWS), :],
                dst_ref=edge_left.at[t],
                send_sem=edge_ss.at[t, 0],
                recv_sem=edge_rs.at[t, 0],
                device_id=(g, member(1)),
                device_id_type=MESH,
            ),
            pltpu.make_async_remote_copy(
                src_ref=fq.at[t, 0, pl.ds(0, ROWS), :],
                dst_ref=edge_right.at[t],
                send_sem=edge_ss.at[t, 1],
                recv_sem=edge_rs.at[t, 1],
                device_id=(g, member(-1)),
                device_id_type=MESH,
            ),
        )

    def halo_copies(t):
        out = []
        for i, (dr, dc) in enumerate(AROUND):
            if dr == 0:
                src = side_send.at[t, i - 2]
                dst = halo_col.at[t, i - 2]
            else:
                edge = pl.ds(0 if dr < 0 else rows - ROWS, ROWS)
                if dc == 0:
                    src = fields.at[t, :, edge, :]
                    dst = halo_row.at[t, i]
                else:
                    src = fields.at[t, :, edge, pl.ds(0 if dc < 0 else cols - LANES, LANES)]
                    dst = halo_col.at[t, i - 2]
            out.append(
                pltpu.make_async_remote_copy(
                    src_ref=src,
                    dst_ref=dst,
                    send_sem=halo_ss.at[t, i],
                    recv_sem=halo_rs.at[t, i],
                    device_id=neighbour((dr, dc)),
                    device_id_type=MESH,
                )
            )
        return out

    fields[0, 0] = state_ref[0]
    sat[...] = state_ref[1]
    fq[0] = frac_ref[...]

    def cell_hots(o, carry):
        index = cell_ref[pl.ds(o, 1), :]
        col_hot[:, lanes(o, cap)] = one_hot(lax.rem(index, cols), cols)
        row_hot[:, lanes(o, cap)] = one_hot(lax.div(index, cols), rows)
        return carry

    lax.fori_loop(0, members, cell_hots, 0)

    each(lambda k: stat_copy(k).wait_recv())

    def seg_hots(o, carry):
        index = stat_recv[1:2, lanes(o, cap)].astype(jnp.int32)
        low_hot[:, lanes(o, cap)] = one_hot(lax.rem(index, LANES), LANES)
        high_hot[:, lanes(o, cap)] = one_hot(lax.div(index, LANES), seg_rows)
        return carry

    lax.fori_loop(0, members, seg_hots, 0)

    def gather_segments(t):
        for copy in edge_copies(t):
            copy.start()
        table = jnp.concatenate(
            [jnp.concatenate(pieces(fq[t, f]), axis=1) for f in range(2)], axis=0
        )

        def body(k, carry):
            here = lanes(member(k), cap)
            low = low_hot[:, here]
            picked = jnp.dot(
                table, jnp.concatenate([low, low], axis=0), preferred_element_type=F32
            )
            high = high_hot[:, here].astype(F32)
            for f in range(2):
                value = jnp.sum(
                    picked[f * seg_rows : (f + 1) * seg_rows] * high, axis=0, keepdims=True
                )
                f_send[t, f : f + 1, here] = value

                @pl.when(k == 0)
                def _():
                    f_recv[t, f : f + 1, here] = value

            @pl.when(k > 0)
            def _():
                f_copy(t, k).start()

            return carry

        lax.fori_loop(0, members, body, 0)

    def gather_cells(t):
        table = jnp.concatenate(pieces(fields[t, 0]) + pieces(sat[...]), axis=0)

        def body(k, carry):
            here = lanes(member(k), cap)
            picked = jnp.dot(table, col_hot[:, here], preferred_element_type=F32)
            hot = row_hot[:, here].astype(F32)
            for f in range(2):
                both = (
                    picked[2 * f * rows : (2 * f + 1) * rows]
                    + picked[(2 * f + 1) * rows : (2 * f + 2) * rows]
                )
                value = jnp.sum(both * hot, axis=0, keepdims=True)
                p_send[t, f : f + 1, here] = value

                @pl.when(k == 0)
                def _():
                    p_recv[t, f : f + 1, here] = value

            @pl.when(k > 0)
            def _():
                p_copy(t, k).start()

            return carry

        lax.fori_loop(0, members, body, 0)

    def collect(acc, hot_rows, hot_cols, values_of):
        acc[...] = jnp.zeros_like(acc)

        def body(j, carry):
            here = lanes(j, group)
            left = spread(hot_rows[:, here], values_of(here))
            acc[...] += lax.dot_general(
                left, hot_cols[:, here], (((1,), (1,)), ((), ())), preferred_element_type=F32
            )
            return carry

        lax.fori_loop(0, slots // group, body, 0)
        height = hot_rows.shape[0]
        return [
            acc[2 * f * height : (2 * f + 1) * height]
            + acc[(2 * f + 1) * height : (2 * f + 2) * height]
            for f in range(3)
        ]

    def scatter_cells(t):
        def values_of(here):
            seg_p = f_recv[t, 0:1, here]
            weight, water = flux_terms(
                stat_send[0:1, here],
                stat_send[pl.ds(2 + t, 1), here],
                p_send[t, 0:1, here],
                p_send[t, 1:2, here],
                seg_p,
                f_recv[t, 1:2, here],
            )
            return weight, weight * seg_p, water

        couple, source, lost = collect(cell_acc, row_hot, col_hot, values_of)
        perm = perm_ref[...]
        p = fields[t, 0]
        inverse = 1.0 / (4.0 + perm + couple)
        scaled = inverse * (perm * p + source)
        sat[...] = sat[...] - TAU_STEP * lost / (perm + couple)
        fields[t, 1] = inverse
        fields[t, 2] = scaled
        for f, field in enumerate((p, inverse, scaled)):
            side_send[t, 0, f] = jnp.transpose(field[:, :LANES])[:ROWS]
            side_send[t, 1, f] = jnp.transpose(field[:, cols - LANES :])[LANES - ROWS :]

    def scatter_segments(t):
        def values_of(here):
            cell_p = p_recv[t, 0:1, here]
            weight, water = flux_terms(
                stat_recv[0:1, here],
                stat_recv[pl.ds(2 + t, 1), here],
                cell_p,
                p_recv[t, 1:2, here],
                f_send[t, 0:1, here],
                f_send[t, 1:2, here],
            )
            return weight * cell_p, weight, water

        inflow, total, gained = collect(seg_acc, high_hot, low_hot, values_of)
        for copy in edge_copies(t):
            copy.wait_recv()
        aperture = aperture_ref[...]
        p = fq[t, 0]
        first = jnp.where(me > 0, edge_left[t, ROWS - 1 : ROWS, LANES - 1 : LANES], F32(0.0))
        last = jnp.where(me < members - 1, edge_right[t, 0:1, 0:1], F32(0.0))
        lane = lax.broadcasted_iota(jnp.int32, (seg_rows, LANES), 1)
        row = lax.broadcasted_iota(jnp.int32, (seg_rows, LANES), 0)
        turned = pltpu.roll(p, 1, axis=1)
        left = jnp.where(lane == 0, pltpu.roll(turned, 1, axis=0), turned)
        left = jnp.where((lane == 0) & (row == 0), first, left)
        turned = pltpu.roll(p, LANES - 1, axis=1)
        right = jnp.where(lane == LANES - 1, pltpu.roll(turned, seg_rows - 1, axis=0), turned)
        right = jnp.where((lane == LANES - 1) & (row == seg_rows - 1), last, right)
        fq[t + 1, 0] = (aperture * p + inflow + left + right) / (aperture + total + 2.0)
        fq[t + 1, 1] = fq[t, 1] + TAU_STEP * gained / (aperture + total)

    def sweeps(t):
        for copy in halo_copies(t):
            copy.wait_recv()
        inside = {
            -1: jnp.where(g > 0, F32(1.0), F32(0.0)),
            1: jnp.where(g < groups - 1, F32(1.0), F32(0.0)),
            0: F32(1.0),
        }
        beside = {
            -1: jnp.where(me > 0, F32(1.0), F32(0.0)),
            1: jnp.where(me < members - 1, F32(1.0), F32(0.0)),
        }
        corner = {
            (-dr, -dc): i - 2 for i, (dr, dc) in enumerate(AROUND) if dc != 0
        }
        east = lax.broadcasted_iota(jnp.int32, (ROWS, LANES), 1) < LANES // 2
        filler = jnp.zeros((LANES - 2 * ROWS, LANES), F32)
        for f, ext in enumerate((ext_x, ext_inv, ext_c)):
            ext[0:ROWS, 0:cols] = halo_row[t, 1, f] * inside[-1]
            ext[ROWS : ROWS + rows, 0:cols] = fields[t, f]
            ext[ROWS + rows :, 0:cols] = halo_row[t, 0, f] * inside[1]
            for dr, at in ((-1, slice(0, ROWS)), (1, slice(ROWS + rows, rows + 2 * ROWS))):
                ext[at, cols:] = jnp.where(
                    east,
                    halo_col[t, corner[dr, 1], f] * (inside[dr] * beside[1]),
                    halo_col[t, corner[dr, -1], f] * (inside[dr] * beside[-1]),
                )
            ext[ROWS : ROWS + rows, cols:] = jnp.transpose(
                jnp.concatenate(
                    [
                        halo_col[t, corner[0, 1], f] * beside[1],
                        filler,
                        halo_col[t, corner[0, -1], f] * beside[-1],
                    ],
                    axis=0,
                )
            )

        height, width = ext_x.shape
        inverse = ext_inv[...]
        scaled = ext_c[...]

        def residual_of(x):
            around = (
                pltpu.roll(x, 1, axis=0)
                + pltpu.roll(x, height - 1, axis=0)
                + pltpu.roll(x, 1, axis=1)
                + pltpu.roll(x, width - 1, axis=1)
            )
            return inverse * around + (scaled - x)

        centre = 0.5 * (HIGH_BOUND + LOW_BOUND)
        half_width = 0.5 * (HIGH_BOUND - LOW_BOUND)
        scale_ratio = centre / half_width
        ratio_now = 1.0 / scale_ratio
        x = ext_x[...]
        update = residual_of(x) / centre
        for sweep_index in range(SWEEPS):
            x = x + update
            if sweep_index + 1 < SWEEPS:
                ratio_next = 1.0 / (2.0 * scale_ratio - ratio_now)
                update = ratio_next * ratio_now * update + (
                    2.0 * ratio_next / half_width
                ) * residual_of(x)
                ratio_now = ratio_next
        fields[t + 1, 0] = x[ROWS : ROWS + rows, :cols]

    gather_segments(0)

    def outer(t, carry):
        gather_cells(t)
        each(lambda k: f_copy(t, k).wait_recv())
        scatter_cells(t)
        for copy in halo_copies(t):
            copy.start()
        each(lambda k: p_copy(t, k).wait_recv())
        scatter_segments(t)

        @pl.when(t + 1 < ITERS)
        def _():
            gather_segments(t + 1)

        sweeps(t)
        return carry

    lax.fori_loop(0, ITERS, outer, 0)

    matrix_out[0] = fields[ITERS, 0]
    matrix_out[1] = sat[...]
    frac_out[...] = fq[ITERS]

    each(lambda k: stat_copy(k).wait_send())

    def drain(t, carry):
        each(lambda k: p_copy(t, k).wait_send())
        each(lambda k: f_copy(t, k).wait_send())
        for copy in edge_copies(t):
            copy.wait_send()
        for copy in halo_copies(t):
            copy.wait_send()
        return carry

    lax.fori_loop(0, ITERS, drain, 0)


def on_device(
    matrix_state,
    matrix_perm,
    frac_state,
    frac_aperture,
    link_cell,
    link_seg,
    link_trans,
    link_count,
    link_upwind,
):
    groups = lax.axis_size("grp")
    members, cap = link_cell.shape[2:]
    rows, cols = matrix_perm.shape
    segs = frac_aperture.shape[1]
    seg_rows = segs // LANES
    slots = members * cap
    vmem = pl.BlockSpec(memory_space=pltpu.VMEM)
    dma = pltpu.SemaphoreType.DMA
    around = len(AROUND)
    matrix_out, frac_out = pl.pallas_call(
        functools.partial(kernel, groups, members, cap),
        out_shape=(
            jax.ShapeDtypeStruct(matrix_state.shape, F32),
            jax.ShapeDtypeStruct((2, seg_rows, LANES), F32),
        ),
        in_specs=[vmem] * 9,
        out_specs=(vmem, vmem),
        scratch_shapes=[
            pltpu.VMEM((ROWS, slots), F32),
            pltpu.VMEM((ROWS, slots), F32),
            pltpu.VMEM((ITERS, 2, slots), F32),
            pltpu.VMEM((ITERS, 2, slots), F32),
            pltpu.VMEM((ITERS, 2, slots), F32),
            pltpu.VMEM((ITERS, 2, slots), F32),
            pltpu.VMEM((ITERS, ROWS, LANES), F32),
            pltpu.VMEM((ITERS, ROWS, LANES), F32),
            pltpu.VMEM((ITERS + 1, 3, rows, cols), F32),
            pltpu.VMEM((rows, cols), F32),
            pltpu.VMEM((ITERS + 1, 2, seg_rows, LANES), F32),
            pltpu.VMEM((ITERS, 2, 3, ROWS, LANES), F32),
            pltpu.VMEM((ITERS, 2, 3, ROWS, cols), F32),
            pltpu.VMEM((ITERS, 6, 3, ROWS, LANES), F32),
            pltpu.VMEM((cols, slots), BF16),
            pltpu.VMEM((rows, slots), BF16),
            pltpu.VMEM((LANES, slots), BF16),
            pltpu.VMEM((seg_rows, slots), BF16),
            pltpu.VMEM((6 * rows, cols), F32),
            pltpu.VMEM((6 * seg_rows, LANES), F32),
            pltpu.VMEM((rows + 2 * ROWS, cols + LANES), F32),
            pltpu.VMEM((rows + 2 * ROWS, cols + LANES), F32),
            pltpu.VMEM((rows + 2 * ROWS, cols + LANES), F32),
            dma((members,)),
            dma((members,)),
            dma((ITERS, members)),
            dma((ITERS, members)),
            dma((ITERS, members)),
            dma((ITERS, members)),
            dma((ITERS, 2)),
            dma((ITERS, 2)),
            dma((ITERS, around)),
            dma((ITERS, around)),
        ],
        compiler_params=pltpu.CompilerParams(
            collective_id=0, has_side_effects=True, vmem_limit_bytes=48 * 1024 * 1024
        ),
    )(
        matrix_state,
        matrix_perm,
        frac_state.reshape(2, seg_rows, LANES),
        frac_aperture.reshape(seg_rows, LANES),
        link_cell[0, 0],
        link_seg[0, 0],
        link_trans[0, 0],
        link_count[0],
        link_upwind[:, 0, 0],
    )
    return matrix_out, frac_out.reshape(2, 1, segs)


def solution(mesh):
    return jax.shard_map(
        on_device,
        mesh=mesh,
        in_specs=(
            P(None, "grp", "frac"),
            P("grp", "frac"),
            P(None, "grp", "frac"),
            P("grp", "frac"),
            P("grp", "frac", None, None),
            P("grp", "frac", None, None),
            P("grp", "frac", None, None),
            P("grp", "frac", None),
            P(None, "grp", "frac", None, None),
        ),
        out_specs=(P(None, "grp", "frac"), P(None, "grp", "frac")),
        check_vma=False,
    )
```

time: 893 us -> 70.3 us (0.08); the launches traced: 877 us -> 69.8 us
  local copies, waits for them, and re-layouts: 370 us -> 8.38 us
  other arithmetic: 274 us -> 0 us
  starting transfers between devices: 186 us -> 0 us
  Pallas kernels: 0 us -> 60.8 us
  waiting for transfers between devices: 26.2 us -> 0 us
  between operations: 20.9 us -> 0.66 us
    gather x24 -> x0, local copies, waits for them, and re-layouts: 276 us -> none  [the longest x6 69.1 us: on_device(): cell_pressure = pressure.reshape(-1)[cell_flat]]
    scatter-add x6 -> x0, other arithmetic: 163 us -> none  [the longest x3 88.5 us: on_device(): jnp.zeros((3, row_count * column_count), jnp.float32).at[:, cell_flat]]
    ppermute x48 -> x0, starting transfers between devices: 137 us -> none  [the longest x24 99 us: extended(): lax.ppermute(tail, axis, [(i, (i + 1) % count) for i in range(ends)])]
    slice x3 -> x0, other arithmetic: 92 us -> none  [on_device(): source_term = cell_totals[1].reshape(row_count, column_count)]
    pallas_call x0 -> x1, Pallas kernels: none -> 60.8 us  [on_device(): pl.pallas_call(functools.partial(kernel, groups, members, cap), out_shape...]
    slice x34 -> x0, local copies, waits for them, and re-layouts: 51.1 us -> none  [the longest x3 35.7 us: on_device(): inflow = segment_totals[0]]
    all_to_all x4 -> x0, starting transfers between devices: 48.9 us -> none  [the longest x3 42.1 us: on_device(): lax.all_to_all(owner_terms.reshape(3, members, capacity), 'frac', split_a...]
    ppermute x48 -> x0, waiting for transfers between devices: 26.2 us -> none  [the longest x24 17.6 us: extended(): lax.ppermute(head, axis, [((i + 1) % count, i) for i in range(ends)])]
  transfers between devices with their start and end apart: 55 -> 0, of which waited for: 16 -> 0; matrix products, arithmetic and copies ran while one was open for 67% -> 0% of each run, Pallas kernels for 0% -> 0%
where the time goes in v1:
time: 70.3 us; the launch traced here: 69.8 us
  Pallas kernels  60.8 us (86%)
  local copies, waits for them, and re-layouts  8.38 us (12%)
    pallas_call x1, Pallas kernels, on_device(): pl.pallas_call(functools.partial(kernel, groups, members, cap), out_shape...  60.8 us
    unnamed x20, local copies, waits for them, and re-layouts  8.38 us

profile of v1, /device:TPU:1, one launch (start us, length us, event | category | flops | bytes accessed | tf_op | source)
XLA Modules:
  0.0 69.8 jit_solution(7566819199270742885)
XLA Ops:
  0.6 0.0 copy-start.8
  0.6 0.6 copy-done.8
  1.3 0.0 copy-start
  1.3 0.9 %copy-done = f32[2,128,256]{2,1,0:T(8,128)S(1)} copy-done((f32[2,128,256]{2,1,0:T(8,128)S(1)}, f32[2,128,256]{2,1,0:T(8,128)}, u32[]{:S(2)}) %copy-start) | copy-done | bytes 262168
  2.2 0.0 copy-start.1
  2.2 0.9 %copy-done.1 = f32[128,256]{1,0:T(8,128)S(1)} copy-done((f32[128,256]{1,0:T(8,128)S(1)}, f32[128,256]{1,0:T(8,128)}, u32[]{:S(2)}) %copy-start.1) | copy-done | bytes 131096
  3.1 0.0 copy-start.2
  3.1 0.8 %copy-done.2 = f32[2,1,8192]{2,1,0:T(1,128)S(1)} copy-done((f32[2,1,8192]{2,1,0:T(1,128)S(1)}, f32[2,1,8192]{2,1,0:T(1,128)}, u32[]{:S(2)}) %copy-start.2) | copy-done | bytes 65560
  4.0 0.0 copy-start.3
  4.0 0.8 %copy-done.3 = s32[3,1,1,16,256]{4,3,2,1,0:T(8,128)S(1)} copy-done((s32[3,1,1,16,256]{4,3,2,1,0:T(8,128)S(1)}, s32[3,1,1,16,256]{4,3,2,1,0:T(8,128)}, u32[]{:S(2)}) %copy-start.3) | copy-done | bytes 49176
  4.8 0.0 copy-start.4
  4.8 0.8 %copy-done.4 = f32[1,8192]{1,0:T(1,128)S(1)} copy-done((f32[1,8192]{1,0:T(1,128)S(1)}, f32[1,8192]{1,0:T(1,128)}, u32[]{:S(2)}) %copy-start.4) | copy-done | bytes 32792
  5.5 0.0 copy-start.5
  5.5 0.7 %copy-done.5 = s32[1,1,16,256]{3,2,1,0:T(8,128)S(1)} copy-done((s32[1,1,16,256]{3,2,1,0:T(8,128)S(1)}, s32[1,1,16,256]{3,2,1,0:T(8,128)}, u32[]{:S(2)}) %copy-start.5) | copy-done | bytes 16408
  6.3 0.0 copy-start.6
  6.3 0.7 %copy-done.6 = s32[1,1,16,256]{3,2,1,0:T(8,128)S(1)} copy-done((s32[1,1,16,256]{3,2,1,0:T(8,128)S(1)}, s32[1,1,16,256]{3,2,1,0:T(8,128)}, u32[]{:S(2)}) %copy-start.6) | copy-done | bytes 16408
  7.0 0.0 copy-start.7
  7.0 0.7 %copy-done.7 = f32[1,1,16,256]{3,2,1,0:T(8,128)S(1)} copy-done((f32[1,1,16,256]{3,2,1,0:T(8,128)S(1)}, f32[1,1,16,256]{3,2,1,0:T(8,128)}, u32[]{:S(2)}) %copy-start.7) | copy-done | bytes 16408
  7.7 60.8 %shard_map.104 = (f32[2,128,256]{2,1,0:T(8,128)S(1)}, f32[2,64,128]{2,1,0:T(8,128)S(1)}) custom-call(f32[2,128,256]{2,1,0:T(8,128)S(1)} %copy-done, f32[128,256]{1,0:T(8,128)S(1)} %copy-done.1, f32[2,64,128]{2,1,0:T(8,128)S(1)} %bitcast.9, f32[64,128]{1,0:T(8,128)S(1)} %bitcast.11, s32[16,256]{1,0:T(8,128)S(1)} %bitcast.12, s32[16,256]{1,0:T(8,128)S(1)} %bitcast.13, ...), custom_call_target="tpu_custom_call" | custom-call | tf_op jit(solution)/shard_map/pallas_call | solution.py:499
  68.5 0.7 %copy.14 = f32[2,128,256]{2,1,0:T(8,128)} copy(f32[2,128,256]{2,1,0:T(8,128)S(1)} %get-tuple-element.10) | data formatting | bytes 524288
  69.2 0.6 copy.15
Async XLA Ops:
  0.6 0.7 copy-start.8
  1.3 0.9 %copy-start = (f32[2,128,256]{2,1,0:T(8,128)S(1)}, f32[2,128,256]{2,1,0:T(8,128)}, u32[]{:S(2)}) copy-start(f32[2,128,256]{2,1,0:T(8,128)} %state_ref.1) | copy-start | bytes 786436
  2.2 0.9 %copy-start.1 = (f32[128,256]{1,0:T(8,128)S(1)}, f32[128,256]{1,0:T(8,128)}, u32[]{:S(2)}) copy-start(f32[128,256]{1,0:T(8,128)} %perm_ref.1) | copy-start | bytes 393220
  3.1 0.8 %copy-start.2 = (f32[2,1,8192]{2,1,0:T(1,128)S(1)}, f32[2,1,8192]{2,1,0:T(1,128)}, u32[]{:S(2)}) copy-start(f32[2,1,8192]{2,1,0:T(1,128)} %param.11) | copy-start | bytes 196612
  4.0 0.8 %copy-start.3 = (s32[3,1,1,16,256]{4,3,2,1,0:T(8,128)S(1)}, s32[3,1,1,16,256]{4,3,2,1,0:T(8,128)}, u32[]{:S(2)}) copy-start(s32[3,1,1,16,256]{4,3,2,1,0:T(8,128)} %param.17) | copy-start | bytes 147460
  4.8 0.8 %copy-start.4 = (f32[1,8192]{1,0:T(1,128)S(1)}, f32[1,8192]{1,0:T(1,128)}, u32[]{:S(2)}) copy-start(f32[1,8192]{1,0:T(1,128)} %param.12) | copy-start | bytes 98308
  5.5 0.7 %copy-start.5 = (s32[1,1,16,256]{3,2,1,0:T(8,128)S(1)}, s32[1,1,16,256]{3,2,1,0:T(8,128)}, u32[]{:S(2)}) copy-start(s32[1,1,16,256]{3,2,1,0:T(8,128)} %param.13) | copy-start | bytes 49156
  6.3 0.7 %copy-start.6 = (s32[1,1,16,256]{3,2,1,0:T(8,128)S(1)}, s32[1,1,16,256]{3,2,1,0:T(8,128)}, u32[]{:S(2)}) copy-start(s32[1,1,16,256]{3,2,1,0:T(8,128)} %param.14) | copy-start | bytes 49156
  7.0 0.7 %copy-start.7 = (f32[1,1,16,256]{3,2,1,0:T(8,128)S(1)}, f32[1,1,16,256]{3,2,1,0:T(8,128)}, u32[]{:S(2)}) copy-start(f32[1,1,16,256]{3,2,1,0:T(8,128)} %param.15) | copy-start | bytes 49156

commit v2 on v1

--- a/solution.py
+++ b/solution.py
@@ -53,17 +53,24 @@
     groups,
     members,
     cap,
-    state_ref,
+    state_in,
+    perm_in,
+    frac_in,
+    aperture_in,
+    cell_in,
+    seg_in,
+    trans_in,
+    count_in,
+    upwind_in,
+    matrix_out,
+    frac_out,
     perm_ref,
-    frac_ref,
     aperture_ref,
     cell_ref,
     seg_ref,
     trans_ref,
     count_ref,
     upwind_ref,
-    matrix_out,
-    frac_out,
     stat_send,
     stat_recv,
     p_send,
@@ -97,6 +104,7 @@
     edge_rs,
     halo_ss,
     halo_rs,
+    load_sem,
 ):
     g = lax.axis_index("grp")
     me = lax.axis_index("frac")
@@ -111,6 +119,26 @@
     def neighbour(step):
         return (lax.rem(g + step[0] + groups, groups), member(step[1]))
 
+    loads = [
+        pltpu.make_async_copy(src, dst, load_sem.at[i])
+        for i, (src, dst) in enumerate(
+            (
+                (count_in, count_ref),
+                (trans_in, trans_ref),
+                (seg_in, seg_ref),
+                (upwind_in, upwind_ref),
+                (cell_in, cell_ref),
+                (state_in.at[0], fields.at[0, 0]),
+                (state_in.at[1], sat),
+                (frac_in, fq.at[0]),
+                (perm_in, perm_ref),
+                (aperture_in, aperture_ref),
+            )
+        )
+    ]
+    for load in loads:
+        load.start()
+
     barrier = pltpu.get_barrier_semaphore()
     for k in range(1, members):
         pl.semaphore_signal(barrier, inc=1, device_id=(g, member(k)), device_id_type=MESH)
@@ -120,6 +148,9 @@
 
     def lanes(block, width):
         return pl.ds(pl.multiple_of(block * width, width), width)
+
+    for load in loads[:4]:
+        load.wait()
 
     eye = lax.broadcasted_iota(jnp.int32, (members, members), 0) == lax.broadcasted_iota(
         jnp.int32, (members, members), 1
@@ -215,9 +246,8 @@
             )
         return out
 
-    fields[0, 0] = state_ref[0]
-    sat[...] = state_ref[1]
-    fq[0] = frac_ref[...]
+    for load in loads[4:]:
+        load.wait()
 
     def cell_hots(o, carry):
         index = cell_ref[pl.ds(o, 1), :]
@@ -236,6 +266,30 @@
         return carry
 
     lax.fori_loop(0, members, seg_hots, 0)
+
+    def gather(per, table, hot_cols, hot_rows, add, send, recv, copy, t):
+        height = hot_rows.shape[0]
+
+        def body(j, carry):
+            q = lax.rem(lax.div(me, per) + j, members // per)
+            here = lanes(q, per * cap)
+            picked = add(jnp.dot(table, hot_cols(here), preferred_element_type=F32))
+            hot = hot_rows[:, here].astype(F32)
+            for f in range(2):
+                send[t, f : f + 1, here] = jnp.sum(
+                    picked[f * height : (f + 1) * height] * hot, axis=0, keepdims=True
+                )
+            for i in range(per):
+                k = lax.rem(q * per + i - me + members, members)
+
+                @pl.when(k > 0)
+                def _():
+                    copy(t, k).start()
+
+            return carry
+
+        lax.fori_loop(0, members // per, body, 0)
+        recv[t, :, lanes(me, cap)] = send[t, :, lanes(me, cap)]
 
     def gather_segments(t):
         for copy in edge_copies(t):
@@ -244,57 +298,26 @@
             [jnp.concatenate(pieces(fq[t, f]), axis=1) for f in range(2)], axis=0
         )
 
-        def body(k, carry):
-            here = lanes(member(k), cap)
+        def both(here):
             low = low_hot[:, here]
-            picked = jnp.dot(
-                table, jnp.concatenate([low, low], axis=0), preferred_element_type=F32
-            )
-            high = high_hot[:, here].astype(F32)
-            for f in range(2):
-                value = jnp.sum(
-                    picked[f * seg_rows : (f + 1) * seg_rows] * high, axis=0, keepdims=True
-                )
-                f_send[t, f : f + 1, here] = value
-
-                @pl.when(k == 0)
-                def _():
-                    f_recv[t, f : f + 1, here] = value
-
-            @pl.when(k > 0)
-            def _():
-                f_copy(t, k).start()
-
-            return carry
-
-        lax.fori_loop(0, members, body, 0)
+            return jnp.concatenate([low, low], axis=0)
+
+        gather(min(members, 16), table, both, high_hot, lambda x: x, f_send, f_recv, f_copy, t)
 
     def gather_cells(t):
-        table = jnp.concatenate(pieces(fields[t, 0]) + pieces(sat[...]), axis=0)
-
-        def body(k, carry):
-            here = lanes(member(k), cap)
-            picked = jnp.dot(table, col_hot[:, here], preferred_element_type=F32)
-            hot = row_hot[:, here].astype(F32)
-            for f in range(2):
-                both = (
-                    picked[2 * f * rows : (2 * f + 1) * rows]
-                    + picked[(2 * f + 1) * rows : (2 * f + 2) * rows]
-                )
-                value = jnp.sum(both * hot, axis=0, keepdims=True)
-                p_send[t, f : f + 1, here] = value
-
-                @pl.when(k == 0)
-                def _():
-                    p_recv[t, f : f + 1, here] = value
-
-            @pl.when(k > 0)
-            def _():
-                p_copy(t, k).start()
-
-            return carry
-
-        lax.fori_loop(0, members, body, 0)
+        highs, lows = zip(pieces(fields[t, 0]), pieces(sat[...]))
+        table = jnp.concatenate(highs + lows, axis=0)
+        gather(
+            min(members, 4),
+            table,
+            lambda here: col_hot[:, here],
+            row_hot,
+            lambda x: x[: 2 * rows] + x[2 * rows :],
+            p_send,
+            p_recv,
+            p_copy,
+            t,
+        )
 
     def collect(acc, hot_rows, hot_cols, values_of):
         acc[...] = jnp.zeros_like(acc)
@@ -476,6 +499,17 @@
     lax.fori_loop(0, ITERS, drain, 0)
 
 
+def write_out(matrix_in, frac_in, matrix_out, frac_out, sems):
+    copies = (
+        pltpu.make_async_copy(matrix_in, matrix_out, sems.at[0]),
+        pltpu.make_async_copy(frac_in, frac_out, sems.at[1]),
+    )
+    for copy in copies:
+        copy.start()
+    for copy in copies:
+        copy.wait()
+
+
 def on_device(
     matrix_state,
     matrix_perm,
@@ -494,6 +528,7 @@
     seg_rows = segs // LANES
     slots = members * cap
     vmem = pl.BlockSpec(memory_space=pltpu.VMEM)
+    hbm = pl.BlockSpec(memory_space=pltpu.HBM)
     dma = pltpu.SemaphoreType.DMA
     around = len(AROUND)
     matrix_out, frac_out = pl.pallas_call(
@@ -502,9 +537,16 @@
             jax.ShapeDtypeStruct(matrix_state.shape, F32),
             jax.ShapeDtypeStruct((2, seg_rows, LANES), F32),
         ),
-        in_specs=[vmem] * 9,
+        in_specs=[hbm] * 9,
         out_specs=(vmem, vmem),
         scratch_shapes=[
+            pltpu.VMEM((rows, cols), F32),
+            pltpu.VMEM((seg_rows, LANES), F32),
+            pltpu.VMEM((members, cap), jnp.int32),
+            pltpu.VMEM((members, cap), jnp.int32),
+            pltpu.VMEM((members, cap), F32),
+            pltpu.VMEM((1, members), jnp.int32),
+            pltpu.VMEM((ITERS, members, cap), jnp.int32),
             pltpu.VMEM((ROWS, slots), F32),
             pltpu.VMEM((ROWS, slots), F32),
             pltpu.VMEM((ITERS, 2, slots), F32),
@@ -538,21 +580,38 @@
             dma((ITERS, 2)),
             dma((ITERS, around)),
             dma((ITERS, around)),
+            dma((10,)),
         ],
         compiler_params=pltpu.CompilerParams(
-            collective_id=0, has_side_effects=True, vmem_limit_bytes=48 * 1024 * 1024
+            collective_id=0, has_side_effects=True, vmem_limit_bytes=40 * 1024 * 1024
         ),
     )(
-        matrix_state,
-        matrix_perm,
-        frac_state.reshape(2, seg_rows, LANES),
-        frac_aperture.reshape(seg_rows, LANES),
-        link_cell[0, 0],
-        link_seg[0, 0],
-        link_trans[0, 0],
-        link_count[0],
-        link_upwind[:, 0, 0],
+        *(
+            pltpu.with_memory_space_constraint(x, pltpu.HBM)
+            for x in (
+                matrix_state,
+                matrix_perm,
+                frac_state.reshape(2, seg_rows, LANES),
+                frac_aperture.reshape(seg_rows, LANES),
+                link_cell[0, 0],
+                link_seg[0, 0],
+                link_trans[0, 0],
+                link_count[0],
+                link_upwind[:, 0, 0],
+            )
+        )
     )
+    matrix_out, frac_out = pl.pallas_call(
+        write_out,
+        out_shape=(
+            jax.ShapeDtypeStruct(matrix_state.shape, F32),
+            jax.ShapeDtypeStruct((2, seg_rows, LANES), F32),
+        ),
+        in_specs=[vmem] * 2,
+        out_specs=(hbm, hbm),
+        scratch_shapes=[dma((2,))],
+        compiler_params=pltpu.CompilerParams(vmem_limit_bytes=4 * 1024 * 1024),
+    )(matrix_out, frac_out)
     return matrix_out, frac_out.reshape(2, 1, segs)
 
 

time: 70.3 us -> 53.4 us (0.76)
  local copies, waits for them, and re-layouts: 8.38 us -> 0 us
  Pallas kernels: 60.8 us -> 52.7 us
    pallas_call x1, Pallas kernels: 60.8 us -> 51.9 us  [on_device(): pl.pallas_call(functools.partial(kernel, groups, members, cap), out_shape...]
    unnamed x20 -> x0, local copies, waits for them, and re-layouts: 8.38 us -> none
    pallas_call x0 -> x1, Pallas kernels: none -> 0.74 us  [on_device(): pl.pallas_call(write_out, out_shape=(jax.ShapeDtypeStruct(matrix_state.sh...]
where the time goes in v2:
time: 53.4 us; the launch traced here: 53.3 us
  Pallas kernels  52.7 us (99%)
  between operations  0.64 us (1%)
    pallas_call x1, Pallas kernels, on_device(): pl.pallas_call(functools.partial(kernel, groups, members, cap), out_shape...  51.9 us

profile of v2, /device:TPU:1, one launch (start us, length us, event | category | flops | bytes accessed | tf_op | source)
XLA Modules:
  0.0 53.3 jit_solution(15008391344484209274)
XLA Ops:
  0.6 51.9 %shard_map.104 = (f32[2,128,256]{2,1,0:T(8,128)S(1)}, f32[2,64,128]{2,1,0:T(8,128)S(1)}) custom-call(f32[2,128,256]{2,1,0:T(8,128)} %state_in.1, f32[128,256]{1,0:T(8,128)} %perm_in.1, f32[2,64,128]{2,1,0:T(8,128)} %bitcast.8, f32[64,128]{1,0:T(8,128)} %bitcast.10, s32[16,256]{1,0:T(8,128)} %bitcast.11, s32[16,256]{1,0:T(8,128)} %bitcast.12, ...), custom_call_target="tpu_custom_call" | custom-call | tf_op jit(solution)/shard_map/pallas_call | solution.py:534
  52.6 0.7 %shard_map.105 = (f32[2,128,256]{2,1,0:T(8,128)}, f32[2,64,128]{2,1,0:T(8,128)}) custom-call(f32[2,128,256]{2,1,0:T(8,128)S(1)} %get-tuple-element.6.matrix_in, f32[2,64,128]{2,1,0:T(8,128)S(1)} %get-tuple-element.7.frac_in), custom_call_target="tpu_custom_call" | custom-call | tf_op jit(solution)/shard_map/pallas_call | solution.py:604

commit v3 on v2

--- a/solution.py
+++ b/solution.py
@@ -77,8 +77,7 @@
     p_recv,
     f_send,
     f_recv,
-    edge_left,
-    edge_right,
+    edges,
     fields,
     sat,
     fq,
@@ -186,13 +185,43 @@
         )
 
     def stat_copy(k):
-        return exchange(stat_send, stat_recv, stat_ss.at[k], stat_rs.at[k], k)
+        return exchange(stat_send, stat_recv, stat_ss, stat_rs, k)
 
     def p_copy(t, k):
-        return exchange(p_send.at[t], p_recv.at[t], p_ss.at[t, k], p_rs.at[t, k], k)
+        return exchange(p_send.at[t], p_recv.at[t], p_ss.at[t], p_rs.at[t], k)
 
     def f_copy(t, k):
-        return exchange(f_send.at[t], f_recv.at[t], f_ss.at[t, k], f_rs.at[t, k], k)
+        return exchange(f_send.at[t], f_recv.at[t], f_ss.at[t], f_rs.at[t], k)
+
+    def total(ref, send_sem, recv_sem):
+        return pltpu.make_async_remote_copy(
+            src_ref=ref,
+            dst_ref=ref,
+            send_sem=send_sem,
+            recv_sem=recv_sem,
+            device_id=(g, member(1)),
+            device_id_type=MESH,
+        )
+
+    others = slots - cap
+
+    def stat_all():
+        return total(stat_recv.at[:, :others], stat_ss, stat_rs)
+
+    def p_all(t):
+        return total(p_recv.at[t, :, :others], p_ss.at[t], p_rs.at[t])
+
+    def f_all(t):
+        return total(f_recv.at[t, :, :others], f_ss.at[t], f_rs.at[t])
+
+    def edge_all(t):
+        return total(edges.at[t], edge_ss.at[t], edge_rs.at[t])
+
+    def halo_all(t):
+        return (
+            total(halo_row.at[t], halo_ss.at[t, 0], halo_rs.at[t, 0]),
+            total(halo_col.at[t], halo_ss.at[t, 1], halo_rs.at[t, 1]),
+        )
 
     def each(body):
         lax.fori_loop(1, members, lambda k, c: (body(k), c)[1], 0)
@@ -204,17 +233,17 @@
         return (
             pltpu.make_async_remote_copy(
                 src_ref=fq.at[t, 0, pl.ds(seg_rows - ROWS, ROWS), :],
-                dst_ref=edge_left.at[t],
-                send_sem=edge_ss.at[t, 0],
-                recv_sem=edge_rs.at[t, 0],
+                dst_ref=edges.at[t, 0],
+                send_sem=edge_ss.at[t],
+                recv_sem=edge_rs.at[t],
                 device_id=(g, member(1)),
                 device_id_type=MESH,
             ),
             pltpu.make_async_remote_copy(
                 src_ref=fq.at[t, 0, pl.ds(0, ROWS), :],
-                dst_ref=edge_right.at[t],
-                send_sem=edge_ss.at[t, 1],
-                recv_sem=edge_rs.at[t, 1],
+                dst_ref=edges.at[t, 1],
+                send_sem=edge_ss.at[t],
+                recv_sem=edge_rs.at[t],
                 device_id=(g, member(-1)),
                 device_id_type=MESH,
             ),
@@ -223,6 +252,7 @@
     def halo_copies(t):
         out = []
         for i, (dr, dc) in enumerate(AROUND):
+            kind = 0 if dc == 0 else 1
             if dr == 0:
                 src = side_send.at[t, i - 2]
                 dst = halo_col.at[t, i - 2]
@@ -238,8 +268,8 @@
                 pltpu.make_async_remote_copy(
                     src_ref=src,
                     dst_ref=dst,
-                    send_sem=halo_ss.at[t, i],
-                    recv_sem=halo_rs.at[t, i],
+                    send_sem=halo_ss.at[t, kind],
+                    recv_sem=halo_rs.at[t, kind],
                     device_id=neighbour((dr, dc)),
                     device_id_type=MESH,
                 )
@@ -257,7 +287,7 @@
 
     lax.fori_loop(0, members, cell_hots, 0)
 
-    each(lambda k: stat_copy(k).wait_recv())
+    stat_all().wait_recv()
 
     def seg_hots(o, carry):
         index = stat_recv[1:2, lanes(o, cap)].astype(jnp.int32)
@@ -319,7 +349,7 @@
             t,
         )
 
-    def collect(acc, hot_rows, hot_cols, values_of):
+    def collect(group, acc, hot_rows, hot_cols, values_of):
         acc[...] = jnp.zeros_like(acc)
 
         def body(j, carry):
@@ -351,7 +381,7 @@
             )
             return weight, weight * seg_p, water
 
-        couple, source, lost = collect(cell_acc, row_hot, col_hot, values_of)
+        couple, source, lost = collect(min(slots, 2048), cell_acc, row_hot, col_hot, values_of)
         perm = perm_ref[...]
         p = fields[t, 0]
         inverse = 1.0 / (4.0 + perm + couple)
@@ -376,13 +406,12 @@
             )
             return weight * cell_p, weight, water
 
-        inflow, total, gained = collect(seg_acc, high_hot, low_hot, values_of)
-        for copy in edge_copies(t):
-            copy.wait_recv()
+        inflow, conduct, gained = collect(min(slots, 4096), seg_acc, high_hot, low_hot, values_of)
+        edge_all(t).wait_recv()
         aperture = aperture_ref[...]
         p = fq[t, 0]
-        first = jnp.where(me > 0, edge_left[t, ROWS - 1 : ROWS, LANES - 1 : LANES], F32(0.0))
-        last = jnp.where(me < members - 1, edge_right[t, 0:1, 0:1], F32(0.0))
+        first = jnp.where(me > 0, edges[t, 0, ROWS - 1 : ROWS, LANES - 1 : LANES], F32(0.0))
+        last = jnp.where(me < members - 1, edges[t, 1, 0:1, 0:1], F32(0.0))
         lane = lax.broadcasted_iota(jnp.int32, (seg_rows, LANES), 1)
         row = lax.broadcasted_iota(jnp.int32, (seg_rows, LANES), 0)
         turned = pltpu.roll(p, 1, axis=1)
@@ -391,11 +420,11 @@
         turned = pltpu.roll(p, LANES - 1, axis=1)
         right = jnp.where(lane == LANES - 1, pltpu.roll(turned, seg_rows - 1, axis=0), turned)
         right = jnp.where((lane == LANES - 1) & (row == seg_rows - 1), last, right)
-        fq[t + 1, 0] = (aperture * p + inflow + left + right) / (aperture + total + 2.0)
-        fq[t + 1, 1] = fq[t, 1] + TAU_STEP * gained / (aperture + total)
+        fq[t + 1, 0] = (aperture * p + inflow + left + right) / (aperture + conduct + 2.0)
+        fq[t + 1, 1] = fq[t, 1] + TAU_STEP * gained / (aperture + conduct)
 
     def sweeps(t):
-        for copy in halo_copies(t):
+        for copy in halo_all(t):
             copy.wait_recv()
         inside = {
             -1: jnp.where(g > 0, F32(1.0), F32(0.0)),
@@ -465,11 +494,11 @@
 
     def outer(t, carry):
         gather_cells(t)
-        each(lambda k: f_copy(t, k).wait_recv())
+        f_all(t).wait_recv()
         scatter_cells(t)
         for copy in halo_copies(t):
             copy.start()
-        each(lambda k: p_copy(t, k).wait_recv())
+        p_all(t).wait_recv()
         scatter_segments(t)
 
         @pl.when(t + 1 < ITERS)
@@ -485,14 +514,10 @@
     matrix_out[1] = sat[...]
     frac_out[...] = fq[ITERS]
 
-    each(lambda k: stat_copy(k).wait_send())
+    stat_all().wait_send()
 
     def drain(t, carry):
-        each(lambda k: p_copy(t, k).wait_send())
-        each(lambda k: f_copy(t, k).wait_send())
-        for copy in edge_copies(t):
-            copy.wait_send()
-        for copy in halo_copies(t):
+        for copy in (p_all(t), f_all(t), edge_all(t), *halo_all(t)):
             copy.wait_send()
         return carry
 
@@ -553,8 +578,7 @@
             pltpu.VMEM((ITERS, 2, slots), F32),
             pltpu.VMEM((ITERS, 2, slots), F32),
             pltpu.VMEM((ITERS, 2, slots), F32),
-            pltpu.VMEM((ITERS, ROWS, LANES), F32),
-            pltpu.VMEM((ITERS, ROWS, LANES), F32),
+            pltpu.VMEM((ITERS, 2, ROWS, LANES), F32),
             pltpu.VMEM((ITERS + 1, 3, rows, cols), F32),
             pltpu.VMEM((rows, cols), F32),
             pltpu.VMEM((ITERS + 1, 2, seg_rows, LANES), F32),
@@ -570,16 +594,16 @@
             pltpu.VMEM((rows + 2 * ROWS, cols + LANES), F32),
             pltpu.VMEM((rows + 2 * ROWS, cols + LANES), F32),
             pltpu.VMEM((rows + 2 * ROWS, cols + LANES), F32),
-            dma((members,)),
-            dma((members,)),
-            dma((ITERS, members)),
-            dma((ITERS, members)),
-            dma((ITERS, members)),
-            dma((ITERS, members)),
+            dma(()),
+            dma(()),
+            dma((ITERS,)),
+            dma((ITERS,)),
+            dma((ITERS,)),
+            dma((ITERS,)),
+            dma((ITERS,)),
+            dma((ITERS,)),
             dma((ITERS, 2)),
             dma((ITERS, 2)),
-            dma((ITERS, around)),
-            dma((ITERS, around)),
             dma((10,)),
         ],
         compiler_params=pltpu.CompilerParams(

time: 53.4 us -> 49.1 us (0.919)
  Pallas kernels: 52.7 us -> 48.3 us
    pallas_call x1, Pallas kernels: 51.9 us -> 47.6 us  [on_device(): pl.pallas_call(functools.partial(kernel, groups, members, cap), out_shape...]
where the time goes in v3:
time: 49.1 us; the launch traced here: 48.9 us
  Pallas kernels  48.3 us (98%)
  between operations  0.64 us (1%)
    pallas_call x1, Pallas kernels, on_device(): pl.pallas_call(functools.partial(kernel, groups, members, cap), out_shape...  47.6 us

profile of v3, /device:TPU:1, one launch (start us, length us, event | category | flops | bytes accessed | tf_op | source)
XLA Modules:
  0.0 48.9 jit_solution(6145007022862611256)
XLA Ops:
  0.6 47.6 %shard_map.104 = (f32[2,128,256]{2,1,0:T(8,128)S(1)}, f32[2,64,128]{2,1,0:T(8,128)S(1)}) custom-call(f32[2,128,256]{2,1,0:T(8,128)} %state_in.1, f32[128,256]{1,0:T(8,128)} %perm_in.1, f32[2,64,128]{2,1,0:T(8,128)} %bitcast.8, f32[64,128]{1,0:T(8,128)} %bitcast.10, s32[16,256]{1,0:T(8,128)} %bitcast.11, s32[16,256]{1,0:T(8,128)} %bitcast.12, ...), custom_call_target="tpu_custom_call" | custom-call | tf_op jit(solution)/shard_map/pallas_call | solution.py:559
  48.2 0.7 %shard_map.105 = (f32[2,128,256]{2,1,0:T(8,128)}, f32[2,64,128]{2,1,0:T(8,128)}) custom-call(f32[2,128,256]{2,1,0:T(8,128)S(1)} %get-tuple-element.6.matrix_in, f32[2,64,128]{2,1,0:T(8,128)S(1)} %get-tuple-element.7.frac_in), custom_call_target="tpu_custom_call" | custom-call | tf_op jit(solution)/shard_map/pallas_call | solution.py:628

commit v4 on v3

--- a/solution.py
+++ b/solution.py
@@ -18,6 +18,8 @@
 BF16 = jnp.bfloat16
 MESH = pl.DeviceIdType.MESH
 LANES = 128
+WIDE = 2048
+PER = 4
 ROWS = 8
 AROUND = ((-1, 0), (1, 0), (0, -1), (0, 1), (-1, -1), (-1, 1), (1, -1), (1, 1))
 
@@ -71,8 +73,8 @@
     trans_ref,
     count_ref,
     upwind_ref,
-    stat_send,
-    stat_recv,
+    seg_send,
+    seg_recv,
     p_send,
     p_recv,
     f_send,
@@ -89,12 +91,14 @@
     low_hot,
     high_hot,
     cell_acc,
+    lost_acc,
     seg_acc,
+    held,
     ext_x,
     ext_inv,
     ext_c,
-    stat_ss,
-    stat_rs,
+    seg_ss,
+    seg_rs,
     p_ss,
     p_rs,
     f_ss,
@@ -110,7 +114,15 @@
     slots = members * cap
     rows, cols = perm_ref.shape
     seg_rows = aperture_ref.shape[0]
-    group = min(slots, 4 * cap)
+    per = min(members, PER)
+    lines = members // per
+    mine = lax.div(me, per)
+
+    def nearest(j):
+        return j + (j // 2) * (1 - 2 * (j % 2)) if lines == 4 else j
+
+    def line(step):
+        return lax.rem(mine + step + lines, lines)
 
     def member(step):
         return lax.rem(me + step + members, members)
@@ -122,11 +134,11 @@
         pltpu.make_async_copy(src, dst, load_sem.at[i])
         for i, (src, dst) in enumerate(
             (
+                (seg_in, seg_ref),
+                (cell_in, cell_ref),
                 (count_in, count_ref),
                 (trans_in, trans_ref),
-                (seg_in, seg_ref),
                 (upwind_in, upwind_ref),
-                (cell_in, cell_ref),
                 (state_in.at[0], fields.at[0, 0]),
                 (state_in.at[1], sat),
                 (frac_in, fq.at[0]),
@@ -148,9 +160,85 @@
     def lanes(block, width):
         return pl.ds(pl.multiple_of(block * width, width), width)
 
-    for load in loads[:4]:
+    loads[0].wait()
+    seg_float = seg_ref[...].astype(F32)
+    for o in range(members):
+        seg_send[0:1, o * cap : (o + 1) * cap] = seg_float[o : o + 1, :]
+
+    pl.semaphore_wait(barrier, members - 1 + len(apart))
+
+    def distance(k):
+        return lax.rem(lax.div(member(k), per) - mine + lines, lines)
+
+    def exchange(send, recv, send_sem, recv_sem, k):
+        to = member(k)
+        return pltpu.make_async_remote_copy(
+            src_ref=send.at[:, lanes(to, cap)],
+            dst_ref=recv.at[:, lanes(me, cap)],
+            send_sem=send_sem,
+            recv_sem=recv_sem,
+            device_id=(g, to),
+            device_id_type=MESH,
+        )
+
+    def seg_copy(k):
+        return exchange(seg_send, seg_recv, seg_ss, seg_rs.at[distance(k)], k)
+
+    def p_copy(t, k):
+        return exchange(p_send.at[t], p_recv.at[t], p_ss.at[t], p_rs.at[t], k)
+
+    def f_copy(t, k):
+        return exchange(f_send.at[t], f_recv.at[t], f_ss.at[t], f_rs.at[t, distance(k)], k)
+
+    def total(ref, send_sem, recv_sem):
+        return pltpu.make_async_remote_copy(
+            src_ref=ref,
+            dst_ref=ref,
+            send_sem=send_sem,
+            recv_sem=recv_sem,
+            device_id=(g, member(1)),
+            device_id_type=MESH,
+        )
+
+    others = slots - cap
+
+    def seg_all():
+        return total(seg_recv.at[:, :others], seg_ss, seg_rs.at[0])
+
+    def p_all(t):
+        return total(p_recv.at[t, :, :others], p_ss.at[t], p_rs.at[t])
+
+    def f_all(t):
+        return total(f_recv.at[t, :, :others], f_ss.at[t], f_rs.at[t, 0])
+
+    def wait_line(j, recv, send_sem, recv_sems):
+        @pl.when(j == 0)
+        def _():
+            total(recv.at[:, : (per - 1) * cap], send_sem, recv_sems.at[0]).wait_recv()
+
+        if lines > 1:
+
+            @pl.when(j > 0)
+            def _():
+                total(recv.at[:, : per * cap], send_sem, recv_sems.at[nearest(j)]).wait_recv()
+
+    def edge_all(t):
+        return total(edges.at[t], edge_ss.at[t], edge_rs.at[t])
+
+    def halo_all(t):
+        return (
+            total(halo_row.at[t], halo_ss.at[t, 0], halo_rs.at[t, 0]),
+            total(halo_col.at[t], halo_ss.at[t, 1], halo_rs.at[t, 1]),
+        )
+
+    def each(body):
+        lax.fori_loop(1, members, lambda k, c: (body(k), c)[1], 0)
+
+    each(lambda k: seg_copy(k).start())
+    seg_recv[:, lanes(me, cap)] = seg_send[:, lanes(me, cap)]
+
+    for load in loads[1:5]:
         load.wait()
-
     eye = lax.broadcasted_iota(jnp.int32, (members, members), 0) == lax.broadcasted_iota(
         jnp.int32, (members, members), 1
     )
@@ -161,73 +249,12 @@
     )
     place = lax.broadcasted_iota(jnp.int32, (members, cap), 1).astype(F32)
     live_trans = jnp.where(place < counts, trans_ref[...], F32(0.0))
-    seg_float = seg_ref[...].astype(F32)
-    ups = [upwind_ref[t].astype(F32) for t in range(ITERS)]
-    stat_send[...] = jnp.zeros_like(stat_send)
-    for o in range(members):
-        here = slice(o * cap, (o + 1) * cap)
-        stat_send[0:1, here] = live_trans[o : o + 1, :]
-        stat_send[1:2, here] = seg_float[o : o + 1, :]
-        for t in range(ITERS):
-            stat_send[2 + t : 3 + t, here] = ups[t][o : o + 1, :]
-
-    pl.semaphore_wait(barrier, members - 1 + len(apart))
-
-    def exchange(send, recv, send_sem, recv_sem, k):
-        to = member(k)
-        return pltpu.make_async_remote_copy(
-            src_ref=send.at[:, lanes(to, cap)],
-            dst_ref=recv.at[:, lanes(me, cap)],
-            send_sem=send_sem,
-            recv_sem=recv_sem,
-            device_id=(g, to),
-            device_id_type=MESH,
-        )
-
-    def stat_copy(k):
-        return exchange(stat_send, stat_recv, stat_ss, stat_rs, k)
-
-    def p_copy(t, k):
-        return exchange(p_send.at[t], p_recv.at[t], p_ss.at[t], p_rs.at[t], k)
-
-    def f_copy(t, k):
-        return exchange(f_send.at[t], f_recv.at[t], f_ss.at[t], f_rs.at[t], k)
-
-    def total(ref, send_sem, recv_sem):
-        return pltpu.make_async_remote_copy(
-            src_ref=ref,
-            dst_ref=ref,
-            send_sem=send_sem,
-            recv_sem=recv_sem,
-            device_id=(g, member(1)),
-            device_id_type=MESH,
-        )
-
-    others = slots - cap
-
-    def stat_all():
-        return total(stat_recv.at[:, :others], stat_ss, stat_rs)
-
-    def p_all(t):
-        return total(p_recv.at[t, :, :others], p_ss.at[t], p_rs.at[t])
-
-    def f_all(t):
-        return total(f_recv.at[t, :, :others], f_ss.at[t], f_rs.at[t])
-
-    def edge_all(t):
-        return total(edges.at[t], edge_ss.at[t], edge_rs.at[t])
-
-    def halo_all(t):
-        return (
-            total(halo_row.at[t], halo_ss.at[t, 0], halo_rs.at[t, 0]),
-            total(halo_col.at[t], halo_ss.at[t, 1], halo_rs.at[t, 1]),
-        )
-
-    def each(body):
-        lax.fori_loop(1, members, lambda k, c: (body(k), c)[1], 0)
-
-    each(lambda k: stat_copy(k).start())
-    stat_recv[:, lanes(me, cap)] = stat_send[:, lanes(me, cap)]
+    for t in range(ITERS):
+        up = upwind_ref[t].astype(F32)
+        for o in range(members):
+            here = slice(o * cap, (o + 1) * cap)
+            p_send[t, 2:3, here] = up[o : o + 1, :]
+            p_send[t, 3:4, here] = live_trans[o : o + 1, :]
 
     def edge_copies(t):
         return (
@@ -276,7 +303,7 @@
             )
         return out
 
-    for load in loads[4:]:
+    for load in loads[5:]:
         load.wait()
 
     def cell_hots(o, carry):
@@ -287,21 +314,16 @@
 
     lax.fori_loop(0, members, cell_hots, 0)
 
-    stat_all().wait_recv()
-
-    def seg_hots(o, carry):
-        index = stat_recv[1:2, lanes(o, cap)].astype(jnp.int32)
-        low_hot[:, lanes(o, cap)] = one_hot(lax.rem(index, LANES), LANES)
-        high_hot[:, lanes(o, cap)] = one_hot(lax.div(index, LANES), seg_rows)
-        return carry
-
-    lax.fori_loop(0, members, seg_hots, 0)
-
-    def gather(per, table, hot_cols, hot_rows, add, send, recv, copy, t):
+    def gather(per, table, hot_cols, hot_rows, add, send, recv, copy, t, block=None):
         height = hot_rows.shape[0]
 
         def body(j, carry):
-            q = lax.rem(lax.div(me, per) + j, members // per)
+            if block is not None:
+                q = block(j)
+            elif per == members:
+                q = 0
+            else:
+                q = line(nearest(lines - 1 - j))
             here = lanes(q, per * cap)
             picked = add(jnp.dot(table, hot_cols(here), preferred_element_type=F32))
             hot = hot_rows[:, here].astype(F32)
@@ -321,7 +343,7 @@
         lax.fori_loop(0, members // per, body, 0)
         recv[t, :, lanes(me, cap)] = send[t, :, lanes(me, cap)]
 
-    def gather_segments(t):
+    def gather_segments(t, size, block=None):
         for copy in edge_copies(t):
             copy.start()
         table = jnp.concatenate(
@@ -332,13 +354,22 @@
             low = low_hot[:, here]
             return jnp.concatenate([low, low], axis=0)
 
-        gather(min(members, 16), table, both, high_hot, lambda x: x, f_send, f_recv, f_copy, t)
+        gather(size, table, both, high_hot, lambda x: x, f_send, f_recv, f_copy, t, block)
+
+    def next_line(j):
+        wait_line(j, seg_recv, seg_ss, seg_rs)
+        q = line(-nearest(j))
+        here = lanes(q, per * cap)
+        index = seg_recv[:, here].astype(jnp.int32)
+        low_hot[:, here] = one_hot(lax.rem(index, LANES), LANES)
+        high_hot[:, here] = one_hot(lax.div(index, LANES), seg_rows)
+        return q
 
     def gather_cells(t):
         highs, lows = zip(pieces(fields[t, 0]), pieces(sat[...]))
         table = jnp.concatenate(highs + lows, axis=0)
         gather(
-            min(members, 4),
+            per,
             table,
             lambda here: col_hot[:, here],
             row_hot,
@@ -349,64 +380,77 @@
             t,
         )
 
-    def collect(group, acc, hot_rows, hot_cols, values_of):
+    def collect(width, acc, hot_rows, hot_cols, values_of, block=lambda j: j):
         acc[...] = jnp.zeros_like(acc)
 
         def body(j, carry):
-            here = lanes(j, group)
+            here = lanes(block(j), width)
             left = spread(hot_rows[:, here], values_of(here))
             acc[...] += lax.dot_general(
                 left, hot_cols[:, here], (((1,), (1,)), ((), ())), preferred_element_type=F32
             )
             return carry
 
-        lax.fori_loop(0, slots // group, body, 0)
+        lax.fori_loop(0, slots // width, body, 0)
         height = hot_rows.shape[0]
         return [
             acc[2 * f * height : (2 * f + 1) * height]
             + acc[(2 * f + 1) * height : (2 * f + 2) * height]
-            for f in range(3)
+            for f in range(acc.shape[0] // (2 * height))
         ]
+
+    def terms(cell_side, seg_side, t, here):
+        cell_p = cell_side[t, 0:1, here]
+        seg_p = seg_side[t, 0:1, here]
+        weight, water = flux_terms(
+            cell_side[t, 3:4, here],
+            cell_side[t, 2:3, here],
+            cell_p,
+            cell_side[t, 1:2, here],
+            seg_p,
+            seg_side[t, 1:2, here],
+        )
+        return cell_p, seg_p, weight, water
 
     def scatter_cells(t):
         def values_of(here):
-            seg_p = f_recv[t, 0:1, here]
-            weight, water = flux_terms(
-                stat_send[0:1, here],
-                stat_send[pl.ds(2 + t, 1), here],
-                p_send[t, 0:1, here],
-                p_send[t, 1:2, here],
-                seg_p,
-                f_recv[t, 1:2, here],
-            )
-            return weight, weight * seg_p, water
-
-        couple, source, lost = collect(min(slots, 2048), cell_acc, row_hot, col_hot, values_of)
+            _, seg_p, weight, _ = terms(p_send, f_recv, t, here)
+            return weight, weight * seg_p
+
+        def arrived(j):
+            wait_line(j, f_recv.at[t], f_ss.at[t], f_rs.at[t])
+            return line(-nearest(j))
+
+        couple, source = collect(per * cap, cell_acc, row_hot, col_hot, values_of, arrived)
         perm = perm_ref[...]
         p = fields[t, 0]
         inverse = 1.0 / (4.0 + perm + couple)
         scaled = inverse * (perm * p + source)
-        sat[...] = sat[...] - TAU_STEP * lost / (perm + couple)
+        held[...] = perm + couple
         fields[t, 1] = inverse
         fields[t, 2] = scaled
+        copies = halo_copies(t)
+        for copy in copies[:2] + copies[4:]:
+            copy.start()
         for f, field in enumerate((p, inverse, scaled)):
             side_send[t, 0, f] = jnp.transpose(field[:, :LANES])[:ROWS]
             side_send[t, 1, f] = jnp.transpose(field[:, cols - LANES :])[LANES - ROWS :]
+        for copy in copies[2:4]:
+            copy.start()
+
+    def scatter_lost(t):
+        def values_of(here):
+            return (terms(p_send, f_recv, t, here)[3],)
+
+        (lost,) = collect(min(slots, WIDE), lost_acc, row_hot, col_hot, values_of)
+        sat[...] = sat[...] - TAU_STEP * lost / held[...]
 
     def scatter_segments(t):
         def values_of(here):
-            cell_p = p_recv[t, 0:1, here]
-            weight, water = flux_terms(
-                stat_recv[0:1, here],
-                stat_recv[pl.ds(2 + t, 1), here],
-                cell_p,
-                p_recv[t, 1:2, here],
-                f_send[t, 0:1, here],
-                f_send[t, 1:2, here],
-            )
+            cell_p, _, weight, water = terms(p_recv, f_send, t, here)
             return weight * cell_p, weight, water
 
-        inflow, conduct, gained = collect(min(slots, 4096), seg_acc, high_hot, low_hot, values_of)
+        inflow, conduct, gained = collect(slots, seg_acc, high_hot, low_hot, values_of)
         edge_all(t).wait_recv()
         aperture = aperture_ref[...]
         p = fq[t, 0]
@@ -490,22 +534,25 @@
                 ratio_now = ratio_next
         fields[t + 1, 0] = x[ROWS : ROWS + rows, :cols]
 
-    gather_segments(0)
+    gather_cells(0)
+    gather_segments(0, per, next_line)
 
     def outer(t, carry):
-        gather_cells(t)
-        f_all(t).wait_recv()
         scatter_cells(t)
-        for copy in halo_copies(t):
-            copy.start()
         p_all(t).wait_recv()
         scatter_segments(t)
 
         @pl.when(t + 1 < ITERS)
         def _():
-            gather_segments(t + 1)
-
+            gather_segments(t + 1, members)
+
+        scatter_lost(t)
         sweeps(t)
+
+        @pl.when(t + 1 < ITERS)
+        def _():
+            gather_cells(t + 1)
+
         return carry
 
     lax.fori_loop(0, ITERS, outer, 0)
@@ -514,7 +561,7 @@
     matrix_out[1] = sat[...]
     frac_out[...] = fq[ITERS]
 
-    stat_all().wait_send()
+    seg_all().wait_send()
 
     def drain(t, carry):
         for copy in (p_all(t), f_all(t), edge_all(t), *halo_all(t)):
@@ -552,6 +599,7 @@
     segs = frac_aperture.shape[1]
     seg_rows = segs // LANES
     slots = members * cap
+    lines = max(1, members // PER)
     vmem = pl.BlockSpec(memory_space=pltpu.VMEM)
     hbm = pl.BlockSpec(memory_space=pltpu.HBM)
     dma = pltpu.SemaphoreType.DMA
@@ -572,10 +620,10 @@
             pltpu.VMEM((members, cap), F32),
             pltpu.VMEM((1, members), jnp.int32),
             pltpu.VMEM((ITERS, members, cap), jnp.int32),
-            pltpu.VMEM((ROWS, slots), F32),
-            pltpu.VMEM((ROWS, slots), F32),
-            pltpu.VMEM((ITERS, 2, slots), F32),
-            pltpu.VMEM((ITERS, 2, slots), F32),
+            pltpu.VMEM((1, slots), F32),
+            pltpu.VMEM((1, slots), F32),
+            pltpu.VMEM((ITERS, 4, slots), F32),
+            pltpu.VMEM((ITERS, 4, slots), F32),
             pltpu.VMEM((ITERS, 2, slots), F32),
             pltpu.VMEM((ITERS, 2, slots), F32),
             pltpu.VMEM((ITERS, 2, ROWS, LANES), F32),
@@ -589,17 +637,19 @@
             pltpu.VMEM((rows, slots), BF16),
             pltpu.VMEM((LANES, slots), BF16),
             pltpu.VMEM((seg_rows, slots), BF16),
-            pltpu.VMEM((6 * rows, cols), F32),
+            pltpu.VMEM((4 * rows, cols), F32),
+            pltpu.VMEM((2 * rows, cols), F32),
             pltpu.VMEM((6 * seg_rows, LANES), F32),
+            pltpu.VMEM((rows, cols), F32),
             pltpu.VMEM((rows + 2 * ROWS, cols + LANES), F32),
             pltpu.VMEM((rows + 2 * ROWS, cols + LANES), F32),
             pltpu.VMEM((rows + 2 * ROWS, cols + LANES), F32),
             dma(()),
-            dma(()),
+            dma((lines,)),
             dma((ITERS,)),
             dma((ITERS,)),
             dma((ITERS,)),
-            dma((ITERS,)),
+            dma((ITERS, lines)),
             dma((ITERS,)),
             dma((ITERS,)),
             dma((ITERS, 2)),

time: 49.1 us -> 46.6 us (0.949)
  Pallas kernels: 48.3 us -> 45.8 us
    pallas_call x1, Pallas kernels: 47.6 us -> 45 us  [on_device(): pl.pallas_call(functools.partial(kernel, groups, members, cap), out_shape...]
where the time goes in v4:
time: 46.6 us; the launch traced here: 46.4 us
  Pallas kernels  45.8 us (98%)
  between operations  0.64 us (1%)
    pallas_call x1, Pallas kernels, on_device(): pl.pallas_call(functools.partial(kernel, groups, members, cap), out_shape...  45 us

profile of v4, /device:TPU:1, one launch (start us, length us, event | category | flops | bytes accessed | tf_op | source)
XLA Modules:
  0.0 46.4 jit_solution(5129626653747481444)
XLA Ops:
  0.6 45.0 %shard_map.104 = (f32[2,128,256]{2,1,0:T(8,128)S(1)}, f32[2,64,128]{2,1,0:T(8,128)S(1)}) custom-call(f32[2,128,256]{2,1,0:T(8,128)} %state_in.1, f32[128,256]{1,0:T(8,128)} %perm_in.1, f32[2,64,128]{2,1,0:T(8,128)} %bitcast.8, f32[64,128]{1,0:T(8,128)} %bitcast.10, s32[16,256]{1,0:T(8,128)} %bitcast.11, s32[16,256]{1,0:T(8,128)} %bitcast.12, ...), custom_call_target="tpu_custom_call" | custom-call | tf_op jit(solution)/shard_map/pallas_call | solution.py:607
  45.7 0.7 %shard_map.105 = (f32[2,128,256]{2,1,0:T(8,128)}, f32[2,64,128]{2,1,0:T(8,128)}) custom-call(f32[2,128,256]{2,1,0:T(8,128)S(1)} %get-tuple-element.6.matrix_in, f32[2,64,128]{2,1,0:T(8,128)S(1)} %get-tuple-element.7.frac_in), custom_call_target="tpu_custom_call" | custom-call | tf_op jit(solution)/shard_map/pallas_call | solution.py:678

commit v5 on v4

--- a/solution.py
+++ b/solution.py
@@ -340,7 +340,7 @@
 
             return carry
 
-        lax.fori_loop(0, members // per, body, 0)
+        lax.fori_loop(0, members // per, body, 0, unroll=True)
         recv[t, :, lanes(me, cap)] = send[t, :, lanes(me, cap)]
 
     def gather_segments(t, size, block=None):
@@ -468,6 +468,8 @@
         fq[t + 1, 1] = fq[t, 1] + TAU_STEP * gained / (aperture + conduct)
 
     def sweeps(t):
+        for f, ext in enumerate((ext_x, ext_inv, ext_c)):
+            ext[ROWS : ROWS + rows, 0:cols] = fields[t, f]
         for copy in halo_all(t):
             copy.wait_recv()
         inside = {
@@ -486,7 +488,6 @@
         filler = jnp.zeros((LANES - 2 * ROWS, LANES), F32)
         for f, ext in enumerate((ext_x, ext_inv, ext_c)):
             ext[0:ROWS, 0:cols] = halo_row[t, 1, f] * inside[-1]
-            ext[ROWS : ROWS + rows, 0:cols] = fields[t, f]
             ext[ROWS + rows :, 0:cols] = halo_row[t, 0, f] * inside[1]
             for dr, at in ((-1, slice(0, ROWS)), (1, slice(ROWS + rows, rows + 2 * ROWS))):
                 ext[at, cols:] = jnp.where(
@@ -555,7 +556,8 @@
 
         return carry
 
-    lax.fori_loop(0, ITERS, outer, 0)
+    for t in range(ITERS):
+        outer(t, 0)
 
     matrix_out[0] = fields[ITERS, 0]
     matrix_out[1] = sat[...]

time: 46.6 us -> 45.9 us (0.985)
  Pallas kernels: 45.8 us -> 45.1 us
    pallas_call x1, Pallas kernels: 45 us -> 44.3 us  [on_device(): pl.pallas_call(functools.partial(kernel, groups, members, cap), out_shape...]
where the time goes in v5:
time: 45.9 us; the launch traced here: 45.7 us
  Pallas kernels  45.1 us (98%)
  between operations  0.64 us (1%)
    pallas_call x1, Pallas kernels, on_device(): pl.pallas_call(functools.partial(kernel, groups, members, cap), out_shape...  44.3 us

profile of v5, /device:TPU:1, one launch (start us, length us, event | category | flops | bytes accessed | tf_op | source)
XLA Modules:
  0.0 45.7 jit_solution(16867558236000173586)
XLA Ops:
  0.6 44.3 %shard_map.104 = (f32[2,128,256]{2,1,0:T(8,128)S(1)}, f32[2,64,128]{2,1,0:T(8,128)S(1)}) custom-call(f32[2,128,256]{2,1,0:T(8,128)} %state_in.1, f32[128,256]{1,0:T(8,128)} %perm_in.1, f32[2,64,128]{2,1,0:T(8,128)} %bitcast.8, f32[64,128]{1,0:T(8,128)} %bitcast.10, s32[16,256]{1,0:T(8,128)} %bitcast.11, s32[16,256]{1,0:T(8,128)} %bitcast.12, ...), custom_call_target="tpu_custom_call" | custom-call | tf_op jit(solution)/shard_map/pallas_call | solution.py:609
  45.0 0.7 %shard_map.105 = (f32[2,128,256]{2,1,0:T(8,128)}, f32[2,64,128]{2,1,0:T(8,128)}) custom-call(f32[2,128,256]{2,1,0:T(8,128)S(1)} %get-tuple-element.6.matrix_in, f32[2,64,128]{2,1,0:T(8,128)S(1)} %get-tuple-element.7.frac_in), custom_call_target="tpu_custom_call" | custom-call | tf_op jit(solution)/shard_map/pallas_call | solution.py:680

commit v6 on v5

--- a/solution.py
+++ b/solution.py
@@ -18,7 +18,7 @@
 BF16 = jnp.bfloat16
 MESH = pl.DeviceIdType.MESH
 LANES = 128
-WIDE = 2048
+WIDE = 1024
 PER = 4
 ROWS = 8
 AROUND = ((-1, 0), (1, 0), (0, -1), (0, 1), (-1, -1), (-1, 1), (1, -1), (1, 1))

time: 45.9 us -> 45.9 us (level)
  no operation moved by 1% of the time
where the time goes in v6:
time: 45.9 us; the launch traced here: 45.7 us
  Pallas kernels  45.1 us (98%)
  between operations  0.64 us (1%)
    pallas_call x1, Pallas kernels, on_device(): pl.pallas_call(functools.partial(kernel, groups, members, cap), out_shape...  44.3 us

profile of v6, /device:TPU:1, one launch (start us, length us, event | category | flops | bytes accessed | tf_op | source)
XLA Modules:
  0.0 45.7 jit_solution(6305371881009368927)
XLA Ops:
  0.6 44.3 %shard_map.104 = (f32[2,128,256]{2,1,0:T(8,128)S(1)}, f32[2,64,128]{2,1,0:T(8,128)S(1)}) custom-call(f32[2,128,256]{2,1,0:T(8,128)} %state_in.1, f32[128,256]{1,0:T(8,128)} %perm_in.1, f32[2,64,128]{2,1,0:T(8,128)} %bitcast.8, f32[64,128]{1,0:T(8,128)} %bitcast.10, s32[16,256]{1,0:T(8,128)} %bitcast.11, s32[16,256]{1,0:T(8,128)} %bitcast.12, ...), custom_call_target="tpu_custom_call" | custom-call | tf_op jit(solution)/shard_map/pallas_call | solution.py:609
  45.0 0.7 %shard_map.105 = (f32[2,128,256]{2,1,0:T(8,128)}, f32[2,64,128]{2,1,0:T(8,128)}) custom-call(f32[2,128,256]{2,1,0:T(8,128)S(1)} %get-tuple-element.6.matrix_in, f32[2,64,128]{2,1,0:T(8,128)S(1)} %get-tuple-element.7.frac_in), custom_call_target="tpu_custom_call" | custom-call | tf_op jit(solution)/shard_map/pallas_call | solution.py:680
